TPU v7x, 32 devices: a whole 2x2x4 slice. The times are simulated.
32 devices in a mesh: mp: 4 (over y, core), rows: 8 (over z, x).
Axes of the slice: x: 2, y: 2, z: 4, core: 2. Of those that a mesh axis runs over, the one named last changes fastest.
Arguments:
- hidden: bfloat16 [256, 4096], P('rows'), may hold values from -60 to 60
- attn_gain: float32 [4096], replicated, may hold values from 0.3 to 1.7
- w_query: bfloat16 [4096, 4096], P(None, 'mp'), may hold values from -0.09375 to 0.09375
- w_key: bfloat16 [4096, 1024], P(None, 'mp'), may hold values from -0.09375 to 0.09375
- w_value: bfloat16 [4096, 1024], P(None, 'mp'), may hold values from -0.09375 to 0.09375
- w_output: bfloat16 [4096, 4096], P('mp'), may hold values from -0.09375 to 0.09375
- query_gain: float32 [128], replicated, may hold values from 0.5 to 1.5
- key_gain: float32 [128], replicated, may hold values from 0.5 to 1.5
- key_cache: bfloat16 [256, 32, 1024], P('rows', None, 'mp'), may hold values from -730 to 730
- value_cache: bfloat16 [256, 32, 1024], P('rows', None, 'mp'), may hold values from -6 to 6
- lengths: int32 [256], P('rows'), may hold values from 1 to 32
- final_gain: float32 [4096], replicated, may hold values from 0.4 to 1.6
- old_embed: bfloat16 [256, 4096], P('rows'), may hold values from -72 to 72
- slab: bfloat16 [4096, 4096], P('rows', 'mp'), may hold values from -6 to 6
- owners: int32 [4096, 1], P('rows'), may hold values from 0 to 7; in each aligned block of 512 rows (0 to 511, 512 to 1023, ...) at most 128 rows name the same one
Outputs:
- migrated: bfloat16 [8192, 4096], P('rows', 'mp')
Inputs may be any that keep to these rules, and one draw needn't show every extreme that they name: `owners`: in each aligned block of 512 cache rows no owner is named by more than 128 rows.
All inputs are finite; a program needn't handle non-finite values.
Results may differ from a plain program's by a relative error of at most 0.008.
Values may be sent and summed in bfloat16 or wider, within the bound.
A program may use at most 128 MiB of HBM per device.

v0:
```python
import math

import jax
import jax.numpy as jnp
from jax import lax
from jax.sharding import PartitionSpec as P

D = 4096
HEADS = 32
KV_HEADS = 8
HEAD = 128
ITERS = 3


def rotate(values, position):
    half_width = values.shape[-1] // 2
    exponent = 2.0 * jnp.arange(half_width, dtype=jnp.float32) / values.shape[-1]
    frequency = jnp.exp(-exponent * math.log(1000000.0))
    angle = position[:, None, None] * frequency[None, None, :]
    cosine = jnp.cos(angle)
    sine = jnp.sin(angle)
    first = values[..., :half_width]
    second = values[..., half_width:]
    return jnp.concatenate(
        [first * cosine - second * sine, second * cosine + first * sine], axis=-1
    )


def head_norm(values, gain):
    scale = lax.rsqrt(jnp.mean(values * values, axis=-1, keepdims=True) + 1e-06)
    return values * scale * gain


def contract_first(left, right, precision):
    return lax.dot_general(
        left,
        right,
        (((0,), (0,)), ((), ())),
        precision=precision,
        preferred_element_type=jnp.float32,
    )


def local(
    hidden,
    attn_gain,
    w_query,
    w_key,
    w_value,
    w_output,
    query_gain,
    key_gain,
    key_cache,
    value_cache,
    lengths,
    final_gain,
    old_embed,
    slab,
    owners,
):
    docs = hidden.shape[0]
    width = hidden.shape[1]
    kv_local = w_key.shape[1] // HEAD
    group = HEADS // KV_HEADS
    rows_count = lax.axis_size("rows")
    mp_count = lax.axis_size("mp")
    cols = width // mp_count
    highest = lax.Precision.HIGHEST
    hidden32 = hidden.astype(jnp.float32)
    normed = (
        hidden32
        * lax.rsqrt(jnp.mean(hidden32 * hidden32, axis=-1, keepdims=True) + 1e-06)
        * attn_gain
    ).astype(jnp.bfloat16)
    position = lengths.astype(jnp.float32)
    query = jnp.dot(normed, w_query, preferred_element_type=jnp.float32).reshape(
        docs, kv_local * group, HEAD
    )
    query = rotate(head_norm(query, query_gain), position).astype(jnp.bfloat16)
    key_new = jnp.dot(normed, w_key, preferred_element_type=jnp.float32).reshape(
        docs, kv_local, HEAD
    )
    key_new = rotate(head_norm(key_new, key_gain), position).astype(jnp.bfloat16)
    value_new = (
        jnp.dot(normed, w_value, preferred_element_type=jnp.float32)
        .reshape(docs, kv_local, HEAD)
        .astype(jnp.bfloat16)
    )
    query_groups = query.reshape(docs, kv_local, group, HEAD)
    keys = key_cache.reshape(docs, key_cache.shape[1], kv_local, HEAD)
    values = value_cache.reshape(docs, value_cache.shape[1], kv_local, HEAD)
    scale = 1.0 / math.sqrt(HEAD)
    scores = (
        jnp.einsum("akgd,apkd->akgp", query_groups, keys, preferred_element_type=jnp.float32)
        * scale
    )
    own_score = (
        jnp.einsum("akgd,akd->akg", query_groups, key_new, preferred_element_type=jnp.float32)
        * scale
    )
    valid = jnp.arange(keys.shape[1], dtype=jnp.int32)[None, :] < lengths[:, None]
    scores = jnp.where(valid[:, None, None, :], scores, -jnp.inf)
    top = jnp.maximum(jnp.max(scores, axis=-1), own_score)
    expo = jnp.exp(scores - top[..., None])
    own_expo = jnp.exp(own_score - top)
    total = jnp.sum(expo, axis=-1) + own_expo
    weights = (expo / total[..., None]).astype(jnp.bfloat16)
    own_weight = (own_expo / total).astype(jnp.bfloat16)
    attended = jnp.einsum("akgp,apkd->akgd", weights, values, preferred_element_type=jnp.float32)
    attended = (
        attended
        + own_weight.astype(jnp.float32)[..., None] * value_new.astype(jnp.float32)[:, :, None, :]
    )
    attended = attended.reshape(docs, kv_local * group * HEAD).astype(jnp.bfloat16)
    partial_value = jnp.dot(attended, w_output, preferred_element_type=jnp.float32)
    state = hidden32 + lax.psum(partial_value, "mp")
    new_embed = (
        state * lax.rsqrt(jnp.mean(state * state, axis=-1, keepdims=True) + 1e-06) * final_gain
    ).astype(jnp.bfloat16)
    new_cols = lax.dynamic_slice_in_dim(new_embed, lax.axis_index("mp") * cols, cols, 1)
    old_cols = lax.all_to_all(old_embed, "rows", split_axis=1, concat_axis=0, tiled=True)
    block = old_cols
    cross = contract_first(block, lax.all_gather(new_cols, "rows", axis=0, tiled=True), None)
    ridge = 0.125 * D
    old32 = old_cols.astype(jnp.float32)
    ridge_map = jnp.zeros_like(cross)
    residual = cross
    direction = cross

    def column_total(current):
        return lax.psum(jnp.sum(current * current, axis=0), "rows")

    res_sq = column_total(residual)
    for sweep in range(ITERS):
        image_docs, direction_sq = lax.psum(
            (jnp.dot(old32, direction, precision=highest), jnp.sum(direction * direction, axis=0)),
            "rows",
        )
        curvature = jnp.sum(image_docs * image_docs, axis=0) + ridge * direction_sq
        alpha = res_sq / curvature
        ridge_map = ridge_map + alpha * direction
        image = contract_first(old32, image_docs, highest) + ridge * direction
        residual = residual - alpha * image
        if sweep + 1 < ITERS:
            new_sq = column_total(residual)
            direction = residual + new_sq / res_sq * direction
            res_sq = new_sq
    map_b = ridge_map.astype(jnp.bfloat16)
    slab_full = lax.all_gather(slab, "mp", axis=1, tiled=True)
    block = slab_full
    moved = jnp.dot(
        block, lax.all_gather(map_b, "rows", axis=0, tiled=True), preferred_element_type=jnp.float32
    ).astype(jnp.bfloat16)
    capacity = 2 * slab.shape[0] // rows_count
    owner_ids = owners[:, 0]
    onehot = (owner_ids[:, None] == jnp.arange(rows_count, dtype=jnp.int32)[None, :]).astype(
        jnp.int32
    )
    counted = jnp.cumsum(onehot, axis=0)
    slot = jnp.sum((counted - 1) * onehot, axis=-1)
    target = owner_ids * capacity + slot
    outgoing = jnp.zeros((rows_count * capacity, cols), jnp.bfloat16).at[target].set(moved)
    return lax.all_to_all(outgoing, "rows", split_axis=0, concat_axis=0, tiled=True)


def solution(mesh):
    return jax.shard_map(
        local,
        mesh=mesh,
        in_specs=(
            P("rows", None),
            P(),
            P(None, "mp"),
            P(None, "mp"),
            P(None, "mp"),
            P("mp", None),
            P(),
            P(),
            P("rows", None, "mp"),
            P("rows", None, "mp"),
            P("rows"),
            P(),
            P("rows", None),
            P("rows", "mp"),
            P("rows", None),
        ),
        out_specs=P("rows", "mp"),
        check_vma=False,
    )
```

profile of v0, /device:TPU:1, one launch (start us, length us, event | category | flops | bytes accessed | tf_op | source)
XLA Modules:
  0.0 631.6 jit_solution(9964104254023096549)
XLA Ops:
  6.6 0.8 convert_element_type.66
  7.4 0.7 iota_compare_fusion
  8.1 1.1 fusion.15
  9.2 1.5 fusion.35
  10.9 5.0 convolution_bitcast_fusion.3
  16.8 0.3 fusion.27
  17.2 0.6 fusion.39
  18.0 0.3 fusion.24
  18.6 2.1 fusion.12
  20.7 0.3 fusion.11
  21.1 5.8 fusion.40
  26.9 0.7 copy.65
  27.6 6.4 %all-to-all-start = ((bf16[32,8,512]{2,0,1:T(8,128)(2,1)}), bf16[32,8,512]{2,0,1:T(8,128)(2,1)S(1)}, u32[]{:S(2)}, u32[]{:S(2)}) async-start(bf16[32,8,512]{2,0,1:T(8,128)(2,1)} %bitcast.115), calls=%async_computation | async-start | bytes 524288 | tf_op jit(solution)/shard_map/all_to_all | solution.py:121
  34.0 0.7 dynamic-slice
  34.7 26.1 %all-reduce.5.cloned.1.call-done = f32[32,4096]{1,0:T(8,128)} async-done(((f32[32,4096]{1,0:T(8,128)}), f32[32,4096]{1,0:T(8,128)}) %all-reduce.5.cloned.1.call-update) | async-done | bytes 524304 | tf_op jit(solution)/shard_map/psum | solution.py:116
  60.8 1.2 multiply_reduce_fusion.7
  62.2 25.6 %all_gather.9 = bf16[256,1024]{1,0:T(8,128)(2,1)S(1)} all-gather(bf16[32,1024]{1,0:T(8,128)(2,1)S(1)} %fusion.23), channel_id=1, replica_groups=mesh['mp'=4,'rows'=8] {'rows'}, dimensions={0}, use_global_device_ids=true | all-gather | bytes 589824 | tf_op jit(solution)/shard_map/all_gather | solution.py:123
  87.8 0.5 fusion.4
  88.3 1.3 copy-done.2
  89.6 2.8 convolution_bitcast_fusion.2
  92.5 18.2 %psum.67 = f32[1024]{0:T(1024)S(1)} all-reduce(f32[1024]{0:T(1024)S(1)} %get-tuple-element.19), channel_id=1, replica_groups=mesh['mp'=4,'rows'=8] {'rows'}, use_global_device_ids=true, to_apply=%region_11.12 | all-reduce | flops 1024 | bytes 8192 | tf_op jit(solution)/shard_map/psum | solution.py:131
  110.7 66.6 %all-reduce.7.cloned.1.call-done = f32[256,1024]{0,1:T(8,128)} async-done(((f32[256,1024]{0,1:T(8,128)}), f32[256,1024]{0,1:T(8,128)}) %all-reduce.7.cloned.1.call-update) | async-done | bytes 1048592 | tf_op jit(solution)/shard_map/psum | solution.py:135
  177.3 1.4 multiply_reduce_fusion.6
  178.7 4.7 multiply_reduce_fusion.3
  183.4 16.6 %psum.69 = f32[1024]{0:T(1024)S(1)} all-reduce(f32[1024]{0:T(1024)S(1)} %get-tuple-element.21), channel_id=1, replica_groups=mesh['mp'=4,'rows'=8] {'rows'}, use_global_device_ids=true, to_apply=%region_15.16 | all-reduce | flops 1024 | bytes 8192 | tf_op jit(solution)/shard_map/psum | solution.py:131
  200.0 2.8 multiply_reduce_fusion.2
  202.8 1.3 copy-done.1
  204.2 2.8 convolution_bitcast_fusion.1
  207.0 13.8 %psum.71 = f32[1024]{0:T(1024)S(1)} all-reduce(f32[1024]{0:T(1024)S(1)} %get-tuple-element.5), channel_id=1, replica_groups=mesh['mp'=4,'rows'=8] {'rows'}, use_global_device_ids=true, to_apply=%region_19.20 | all-reduce | flops 1024 | bytes 8192 | tf_op jit(solution)/shard_map/psum | solution.py:135
  220.9 65.7 %all-reduce.9.cloned.1.call-done = f32[256,1024]{0,1:T(8,128)} async-done(((f32[256,1024]{0,1:T(8,128)}), f32[256,1024]{0,1:T(8,128)}) %all-reduce.9.cloned.1.call-update) | async-done | bytes 1048592 | tf_op jit(solution)/shard_map/psum | solution.py:135
  286.5 1.4 multiply_reduce_fusion.5
  288.0 5.3 multiply_reduce_fusion.1
  293.3 16.5 %psum.72 = f32[1024]{0:T(1024)S(1)} all-reduce(f32[1024]{0:T(1024)S(1)} %get-tuple-element.23), channel_id=1, replica_groups=mesh['mp'=4,'rows'=8] {'rows'}, use_global_device_ids=true, to_apply=%region_21.22 | all-reduce | flops 1024 | bytes 8192 | tf_op jit(solution)/shard_map/psum | solution.py:131
  309.7 5.1 convolution_bitcast_fusion
  314.9 0.5 all-gather.5.cloned.1.call-update
  315.5 2.6 multiply_reduce_fusion
  318.0 14.4 %psum.74 = f32[1024]{0:T(1024)S(1)} all-reduce(f32[1024]{0:T(1024)S(1)} %multiply_reduce_fusion), channel_id=1, replica_groups=mesh['mp'=4,'rows'=8] {'rows'}, use_global_device_ids=true, to_apply=%region_25.26 | all-reduce | flops 1024 | bytes 8192 | tf_op jit(solution)/shard_map/psum | solution.py:135
  332.4 61.4 %all-reduce.11.cloned.1.call-done = f32[256,1024]{0,1:T(8,128)} async-done(((f32[256,1024]{0,1:T(8,128)}), f32[256,1024]{0,1:T(8,128)}) %all-reduce.11.cloned.1.call-update) | async-done | bytes 1048592 | tf_op jit(solution)/shard_map/psum | solution.py:135
  393.8 1.4 multiply_reduce_fusion.4
  395.3 4.7 fusion.7
  400.1 1.1 reduce-window.6
  401.6 28.9 %all-gather.5.cloned.1.call-done = bf16[512,4096]{1,0:T(8,128)(2,1)} async-done(((bf16[512,1024]{1,0:T(8,128)(2,1)}), bf16[512,4096]{1,0:T(8,128)(2,1)}) %all-gather.5.cloned.1.call-update) | async-done | bytes 4194320 | tf_op jit(solution)/shard_map/all_gather | solution.py:149
  430.5 126.4 %all-gather.3.cloned.1.call-done = bf16[4096,1024]{1,0:T(8,128)(2,1)} async-done(((bf16[512,1024]{1,0:T(8,128)(2,1)}), bf16[4096,1024]{1,0:T(8,128)(2,1)}) %all-gather.3.cloned.1.call-update) | async-done | bytes 8388624 | tf_op jit(solution)/shard_map/all_gather | solution.py:152
  556.9 10.1 %fusion.9 = bf16[512,1024]{0,1:T(8,128)(2,1)} fusion(bf16[4096,1024]{1,0:T(8,128)(2,1)} %all-gather.3.cloned.1.call-done, bf16[512,4096]{1,0:T(8,128)(2,1)} %all-gather.5.cloned.1.call-done), kind=kOutput, calls=%fused_computation.25 | convolution fusion | flops 4295491584 | bytes 13631488 | tf_op jit(solution)/shard_map/dot_general | solution.py:151
  567.0 1.5 copy.45
  568.5 4.1 scatter_custom_fusion
  572.6 50.9 %all_to_all.31 = bf16[8,128,1024]{2,1,0:T(8,128)(2,1)S(1)} all-to-all(bf16[8,128,1024]{2,1,0:T(8,128)(2,1)} %bitcast.122), channel_id=1, replica_groups=mesh['mp'=4,'rows'=8] {'rows'}, dimensions={0} | all-to-all | bytes 4194304 | tf_op jit(solution)/shard_map/all_to_all | solution.py:163
  623.5 1.3 copy.71
  (69 shorter events, 2.4 us)
Async XLA Ops:
  6.5 2.7 copy-start
  6.5 4.3 copy-start.3
  6.5 4.3 copy-start.5
  6.5 54.3 %all-reduce.5.cloned.1.call-start = ((), (), s32[]{:S(2)}) async-start(), calls=%async_computation.2 | async-start | bytes 1048576 | tf_op jit(solution)/shard_map/psum | solution.py:116
  10.9 5.2 copy-start.7
  10.9 5.5 copy-start.8
  10.9 6.3 copy-start.9
  17.7 2.9 copy-start.10
  21.1 5.8 copy-start.4
  27.6 60.2 %all-to-all-start = ((bf16[32,8,512]{2,0,1:T(8,128)(2,1)}), bf16[32,8,512]{2,0,1:T(8,128)(2,1)S(1)}, u32[]{:S(2)}, u32[]{:S(2)}) async-start(bf16[32,8,512]{2,0,1:T(8,128)(2,1)} %bitcast.115), calls=%async_computation | async-start | bytes 524288 | tf_op jit(solution)/shard_map/all_to_all | solution.py:121
  34.0 143.3 %all-reduce.7.cloned.1.call-start = ((), (), s32[]{:S(2)}) async-start(), calls=%async_computation.3 | async-start | bytes 2097152 | tf_op jit(solution)/shard_map/psum | solution.py:135
  88.3 1.3 copy-start.2
  92.5 194.1 %all-reduce.9.cloned.1.call-start = ((), (), s32[]{:S(2)}) async-start(), calls=%async_computation.4 | async-start | bytes 2097152 | tf_op jit(solution)/shard_map/psum | solution.py:135
  202.8 1.4 copy-start.1
  207.0 186.8 %all-reduce.11.cloned.1.call-start = ((), (), s32[]{:S(2)}) async-start(), calls=%async_computation.5 | async-start | bytes 2097152 | tf_op jit(solution)/shard_map/psum | solution.py:135
  314.8 115.7 %all-gather.5.cloned.1.call-start = ((), (), s32[]{:S(2)}) async-start(), calls=%async_computation.7 | async-start | bytes 5242880 | tf_op jit(solution)/shard_map/all_gather | solution.py:149
  315.4 241.5 %all-gather.3.cloned.1.call-start = ((), (), s32[]{:S(2)}) async-start(), calls=%async_computation.6 | async-start | bytes 9437184 | tf_op jit(solution)/shard_map/all_gather | solution.py:152
  395.3 4.8 copy-start.6
Sparse Core Ops, SparseCore 0:
  27.0 33.7 all-reduce.4
  92.6 84.6 all-reduce.6
  207.1 79.3 all-reduce.8
  314.9 78.8 all-reduce.10
  395.3 35.1 all-gather.4
  432.7 124.1 all-gather.2
where the time goes:
time: 634 us; the launch traced here: 632 us
  waiting for transfers between devices  376 us (59%)
  blocking collectives  156 us (25%)
  matrix products  46.8 us (7%)
  other arithmetic  20.8 us (3%)
  between operations  13.9 us (2%)
  local copies, waits for them, and re-layouts  12 us (2%)
  starting transfers between devices  6.56 us (1%)
    psum x3, waiting for transfers between devices, local(): lax.psum((jnp.dot(old32, direction, precision=highest), jnp.sum(direction...  194 us
    all_gather x1, waiting for transfers between devices, local(): lax.all_gather(map_b, 'rows', axis=0, tiled=True)  126 us
    psum x3, blocking collectives, column_total(): return lax.psum(jnp.sum(current * current, axis=0), 'rows')  51.3 us
    all_to_all x1, blocking collectives, local(): lax.all_to_all(outgoing, 'rows', split_axis=0, concat_axis=0, tiled=True)  50.9 us
    all_gather x1, waiting for transfers between devices, local(): slab_full = lax.all_gather(slab, 'mp', axis=1, tiled=True)  28.9 us
    psum x2, blocking collectives, local(): lax.psum((jnp.dot(old32, direction, precision=highest), jnp.sum(direction...  28.2 us
    psum x1, waiting for transfers between devices, local(): state = hidden32 + lax.psum(partial_value, 'mp')  26.1 us
    all_gather x1, blocking collectives, local(): lax.all_gather(new_cols, 'rows', axis=0, tiled=True)  25.6 us
  transfers between devices with their start and end apart: 7, of which 6 were waited for; matrix products, arithmetic and copies ran while one was open for 2% of the time, Pallas kernels for 0%

commit v1 on v0

v1 whole, which is shorter than its diff:
```python
import functools
import math

import jax
import jax.numpy as jnp
from jax import lax
from jax.experimental import pallas as pl
from jax.experimental.pallas import tpu as pltpu
from jax.sharding import PartitionSpec as P

D = 4096
HEADS = 32
KV_HEADS = 8
HEAD = 128
ITERS = 3
MESH = pl.DeviceIdType.MESH
F32 = jnp.float32
BF16 = jnp.bfloat16
CHUNKS = 8


def dot(left, right, left_dim=1, right_dim=0):
    return lax.dot_general(
        left, right, (((left_dim,), (right_dim,)), ((), ())), preferred_element_type=F32
    )


def encode_kernel(
    n_mp, n_rows,
    hidden, attn_gain, w_query, w_key, w_value, w_output, query_gain, key_gain,
    key_cache, value_cache, lengths, final_gain, old_embed, slab, owners,
    new_out, gram_out, routed_out,
    wq, wk, wv, wo, kc, vc, sl, normed, q_acc, k_acc, v_acc, attended,
    part, part_in, part_sum, part_far, sq_own, sq_in, new_all,
    old_all, side, side_in, side_sum, side_far, outgoing, routed, gram,
    load_sem, weight_sem, wo_sem,
    part_a, part_b, sq_sem, new_f, new_n, old_f, old_n, side_a, side_b,
    trip_sem, gram_f, gram_n, routed_f, routed_n, out_sem,
):
    mp = lax.axis_index("mp")
    row = lax.axis_index("rows")
    docs, width = hidden.shape
    cols = width // n_mp
    anchors = n_rows * docs
    share = anchors // n_mp
    slab_rows = slab.shape[0]
    cap = outgoing.shape[2]
    kv_local = k_acc.shape[1] // HEAD
    group = HEADS // KV_HEADS
    ctx = key_cache.shape[0] // docs
    mp_half, rows_half = n_mp // 2, n_rows // 2
    mp_slow, core = mp // 2, mp % 2
    row_slow, row_fast = row // 2, row % 2

    def remote(src, dst, sems, spot, to_mp, to_row):
        return pltpu.make_async_remote_copy(
            src_ref=src, dst_ref=dst, send_sem=sems.at[0, spot], recv_sem=sems.at[1, spot],
            device_id={"mp": to_mp, "rows": to_row}, device_id_type=MESH,
        )

    def far_rows(buf, sems):
        return [
            remote(buf.at[row], buf.at[row], sems, off - 1, mp,
                   ((row_slow + off) % rows_half) * 2 + row_fast)
            for off in range(1, rows_half)
        ]

    def near_rows(buf, sems):
        found = []
        for off in range(rows_half):
            block = ((row_slow + rows_half - off) % rows_half) * 2 + row_fast
            found.append(remote(buf.at[block], buf.at[block], sems, off, mp,
                                row_slow * 2 + 1 - row_fast))
        return found

    def far_mp(buf, sems):
        return [
            remote(buf.at[mp], buf.at[mp], sems, off - 1,
                   ((mp_slow + off) % mp_half) * 2 + core, row)
            for off in range(1, mp_half)
        ]

    def near_mp(buf, sems):
        found = []
        for off in range(mp_half):
            block = ((mp_slow + mp_half - off) % mp_half) * 2 + core
            found.append(remote(buf.at[block], buf.at[block], sems, off,
                                mp_slow * 2 + 1 - core, row))
        return found

    def reduce_far(summed, landed, sems):
        found = []
        for off in range(1, mp_half):
            there = (mp_slow + off) % mp_half
            found.append(remote(summed.at[there], landed.at[off - 1], sems, off - 1,
                                there * 2 + core, row))
        return found

    def start(copies):
        for copy in copies:
            copy.start()

    sent = []

    def received(copies):
        for copy in copies:
            copy.wait_recv()
            sent.append(copy)

    depth = width // CHUNKS

    def weight_copies(step):
        span = pl.ds(pl.multiple_of(step * depth, depth), depth)
        return [
            pltpu.make_async_copy(src.at[span, :], dst.at[span, :], weight_sem.at[i, step])
            for i, (src, dst) in enumerate(((w_query, wq), (w_key, wk), (w_value, wv)))
        ]

    def output_block(step):
        return 2 * (step % mp_half) + lax.rem(core + 1 + step // mp_half, 2)

    def output_copy(step):
        span = pl.ds(pl.multiple_of(output_block(step) * cols, cols), cols)
        return pltpu.make_async_copy(w_output.at[:, span], wo.at[:, span], wo_sem.at[step])

    for step in range(CHUNKS):
        start(weight_copies(step))
    loads = [
        pltpu.make_async_copy(key_cache, kc, load_sem.at[0]),
        pltpu.make_async_copy(value_cache, vc, load_sem.at[1]),
        pltpu.make_async_copy(slab, sl, load_sem.at[2]),
    ]
    start(loads)
    for step in range(n_mp):
        output_copy(step).start()

    barrier = pltpu.get_barrier_semaphore()
    for off in range(1, n_rows):
        pl.semaphore_signal(barrier, inc=1, device_id={"mp": mp, "rows": lax.rem(row + off, n_rows)},
                            device_id_type=MESH)
    for off in range(1, n_mp):
        pl.semaphore_signal(barrier, inc=1, device_id={"mp": lax.rem(mp + off, n_mp), "rows": row},
                            device_id_type=MESH)
    mine = pl.ds(pl.multiple_of(mp * cols, cols), cols)
    old_all[row] = old_embed[:, mine]
    pl.semaphore_wait(barrier, n_rows + n_mp - 2)

    old_far = far_rows(old_all, old_f)
    start(old_far)
    old_near = near_rows(old_all, old_n)
    old_near[0].start()

    hidden32 = hidden[...].astype(F32)
    normed[...] = (
        hidden32 * lax.rsqrt(jnp.mean(hidden32 * hidden32, axis=-1, keepdims=True) + 1e-06)
        * attn_gain[...]
    ).astype(BF16)

    q_acc[...] = jnp.zeros_like(q_acc)
    k_acc[...] = jnp.zeros_like(k_acc)
    v_acc[...] = jnp.zeros_like(v_acc)

    def project(step, carry):
        span = pl.ds(pl.multiple_of(step * depth, depth), depth)
        for copy in weight_copies(step):
            copy.wait()
        piece = normed[:, span]
        q_acc[...] += dot(piece, wq[span, :])
        k_acc[...] += dot(piece, wk[span, :])
        v_acc[...] += dot(piece, wv[span, :])
        return carry

    lax.fori_loop(0, CHUNKS, project, 0)

    tall = group * docs
    spot = lax.broadcasted_iota(jnp.int32, (tall, docs), 0) % docs
    named = lax.broadcasted_iota(jnp.int32, (tall, docs), 1)
    length = jnp.sum(
        jnp.where(spot == named, lengths[...].astype(F32), 0.0), axis=-1, keepdims=True
    )
    lane = lax.broadcasted_iota(jnp.int32, (docs, HEAD), 1)
    half = HEAD // 2
    frequency = jnp.exp(
        -(2.0 * (lane % half).astype(F32) / HEAD) * math.log(1000000.0)
    )
    angle = length[:docs] * frequency
    cosine = jnp.cos(angle)
    sine = jnp.sin(angle) * jnp.where(lane < half, -1.0, 1.0)

    def turned(values, gain):
        scale = lax.rsqrt(jnp.mean(values * values, axis=-1, keepdims=True) + 1e-06)
        values = values * scale * gain
        return (values * cosine + pltpu.roll(values, half, 1) * sine).astype(BF16)

    loads[0].wait()
    loads[1].wait()
    place_row = lax.broadcasted_iota(jnp.int32, (tall, docs * ctx), 0) % docs * ctx
    place_lane = lax.broadcasted_iota(jnp.int32, (tall, docs * ctx), 1)
    valid = (place_lane >= place_row) & (place_lane < place_row + length.astype(jnp.int32))
    for g in range(kv_local):
        span = slice(g * HEAD, (g + 1) * HEAD)
        queries = jnp.concatenate(
            [
                turned(q_acc[:, (g * group + h) * HEAD:(g * group + h + 1) * HEAD], query_gain[...])
                for h in range(group)
            ],
            axis=0,
        )
        key_new = jnp.concatenate([turned(k_acc[:, span], key_gain[...])] * group, axis=0)
        value_new = jnp.concatenate([v_acc[:, span].astype(BF16)] * group, axis=0)
        factor = 1.0 / math.sqrt(HEAD)
        scores = jnp.where(valid, dot(queries, kc[:, span], 1, 1) * factor, -jnp.inf)
        own_score = jnp.sum(
            queries.astype(F32) * key_new.astype(F32), axis=-1, keepdims=True
        ) * factor
        top = jnp.maximum(jnp.max(scores, axis=-1, keepdims=True), own_score)
        expo = jnp.exp(scores - top)
        own_expo = jnp.exp(own_score - top)
        inverse = 1.0 / (jnp.sum(expo, axis=-1, keepdims=True) + own_expo)
        weights = (expo * inverse).astype(BF16)
        own_weight = (own_expo * inverse).astype(BF16).astype(F32)
        mixed = dot(weights, vc[:, span]) + own_weight * value_new.astype(F32)
        for h in range(group):
            attended[:, (g * group + h) * HEAD:(g * group + h + 1) * HEAD] = mixed[
                h * docs:(h + 1) * docs
            ].astype(BF16)

    received(old_far)
    start(old_near[1:])

    def project_out(step, carry):
        output_copy(step).wait()
        block = output_block(step)
        span = pl.ds(pl.multiple_of(block * cols, cols), cols)
        part[block % 2, block // 2] = dot(attended[...], wo[:, span])
        return carry

    lax.fori_loop(0, mp_half, project_out, 0)
    part_near = remote(part.at[1 - core], part_in, part_a, 0, mp_slow * 2 + 1 - core, row)
    part_near.start()
    lax.fori_loop(mp_half, n_mp, project_out, 0)

    received([part_near])
    part_sum[...] = part[core] + part_in[...]
    part_apart = reduce_far(part_sum, part_far, part_b)
    start(part_apart)

    received(old_near)
    loads[2].wait()
    olds = old_all[...].reshape(anchors, cols)
    for right, base in ((sl, 0), (None, slab_rows)):
        product = dot(olds, olds if right is None else right[...], 1, 1)
        for j in range(n_mp):
            side[j % 2, j // 2, :, base:base + product.shape[1]] = product[
                j * share:(j + 1) * share
            ]
    side_near = remote(side.at[1 - core], side_in, side_a, 0, mp_slow * 2 + 1 - core, row)
    side_near.start()

    received(part_apart)
    state = hidden[:, mine].astype(F32) + part_sum[mp_slow]
    for off in range(1, mp_half):
        state = state + part_far[off - 1]
    square = jnp.sum(state * state, axis=-1, keepdims=True)
    sq_own[...] = jnp.broadcast_to(square, sq_own.shape)
    sq_copies = [
        remote(sq_own, sq_in.at[off - 1], sq_sem, off - 1, lax.rem(mp + off, n_mp), row)
        for off in range(1, n_mp)
    ]
    start(sq_copies)

    received([side_near])
    side_sum[...] = side[core] + side_in[...]
    side_apart = reduce_far(side_sum, side_far, side_b)
    start(side_apart)

    received(sq_copies)
    total = sq_own[...]
    for off in range(1, n_mp):
        total = total + sq_in[off - 1]
    scale = lax.rsqrt(total[:, :1] / width + 1e-06)
    new_all[row] = (state * scale * final_gain[:, mine]).astype(BF16)
    new_far = far_rows(new_all, new_f)
    start(new_far)
    new_near = near_rows(new_all, new_n)
    new_near[0].start()

    lanes = lax.broadcasted_iota(jnp.int32, (slab_rows, HEAD), 1)
    chosen = jnp.where(owners[...] == lanes, 1.0, 0.0)
    earlier = jnp.where(
        lax.broadcasted_iota(jnp.int32, (slab_rows, slab_rows), 1)
        < lax.broadcasted_iota(jnp.int32, (slab_rows, slab_rows), 0), 1.0, 0.0
    )
    slot = jnp.sum(
        dot(earlier.astype(BF16), chosen.astype(BF16)) * chosen, axis=-1, keepdims=True
    )
    target = owners[...].astype(F32) * cap + slot

    received(side_apart)
    whole = side_sum[mp_slow]
    for off in range(1, mp_half):
        whole = whole + side_far[off - 1]
    gram[mp] = whole[:, slab_rows:]
    gram_far = far_mp(gram, gram_f)
    start(gram_far)
    gram_near = near_mp(gram, gram_n)
    gram_near[0].start()
    body = whole[:, :slab_rows].astype(BF16)
    seats = lax.broadcasted_iota(jnp.int32, (slab_rows, cap), 1).astype(F32)
    for o in range(n_rows):
        put = jnp.where(target == seats + float(o * cap), 1.0, 0.0).astype(BF16)
        outgoing[o] = dot(body, put).astype(BF16)
    trips = []
    for off in range(1, n_rows):
        there = lax.rem(row + off, n_rows)
        trips.append(remote(outgoing.at[there], routed.at[mp, row], trip_sem, off - 1, mp, there))
    start(trips)
    routed[mp, row] = outgoing[row]

    received(new_far)
    start(new_near[1:])
    received(gram_far)
    start(gram_near[1:])

    received(trips)
    routed_far = far_mp(routed, routed_f)
    start(routed_far)
    routed_near = near_mp(routed, routed_n)
    routed_near[0].start()
    received(routed_far)
    start(routed_near[1:])

    received(gram_near)
    received(new_near)
    outs = [
        pltpu.make_async_copy(gram, gram_out, out_sem.at[0]),
        pltpu.make_async_copy(new_all, new_out, out_sem.at[1]),
    ]
    start(outs)
    received(routed_near)
    outs.append(pltpu.make_async_copy(routed, routed_out, out_sem.at[2]))
    outs[2].start()
    for copy in sent:
        copy.wait_send()
    for copy in outs:
        copy.wait()


def solve_kernel(ridge, targets, gram, routed, out):
    anchors = gram.shape[0]
    n_rows, cap = routed.shape[1], routed.shape[3]
    high = gram[...].astype(BF16)
    low = (gram[...] - high.astype(F32)).astype(BF16)

    def apply(values):
        top = values.astype(BF16)
        rest = (values - top.astype(F32)).astype(BF16)
        return dot(high, top) + (dot(high, rest) + dot(low, top))

    def total(values):
        return jnp.sum(values, axis=0, keepdims=True)

    start = targets[...]
    residual = start.astype(F32)
    direction = residual
    image_docs = dot(high, start) + dot(low, start)
    res_sq = total(residual * image_docs)
    coeffs = jnp.zeros_like(residual)
    for sweep in range(ITERS):
        curvature = total(image_docs * image_docs) + ridge * total(direction * image_docs)
        alpha = res_sq / curvature
        coeffs = coeffs + alpha * direction
        if sweep + 1 < ITERS:
            residual = residual - alpha * (image_docs + ridge * direction)
            spread = apply(residual)
            new_sq = total(residual * spread)
            ratio = new_sq / res_sq
            direction = residual + ratio * direction
            image_docs = spread + ratio * image_docs
            res_sq = new_sq
    top = coeffs.astype(BF16)
    rest = (coeffs - top.astype(F32)).astype(BF16)
    for b in range(n_rows):
        block = routed[:, b].reshape(anchors, cap)
        out[b * cap:(b + 1) * cap, :] = (dot(block, top, 0, 0) + dot(block, rest, 0, 0)).astype(BF16)


def local(
    hidden, attn_gain, w_query, w_key, w_value, w_output, query_gain, key_gain,
    key_cache, value_cache, lengths, final_gain, old_embed, slab, owners,
):
    n_rows = lax.axis_size("rows")
    n_mp = lax.axis_size("mp")
    docs, width = hidden.shape
    cols = width // n_mp
    anchors = n_rows * docs
    share = anchors // n_mp
    slab_rows = slab.shape[0]
    cap = 2 * slab_rows // n_rows
    kv_width = w_key.shape[1]
    q_width = w_query.shape[1]
    mp_half, rows_half = n_mp // 2, n_rows // 2
    key_cache = key_cache.reshape(-1, kv_width)
    value_cache = value_cache.reshape(-1, kv_width)
    side_width = slab_rows + anchors
    far_mp, far_rows = max(mp_half - 1, 1), max(rows_half - 1, 1)
    hbm = pl.BlockSpec(memory_space=pl.ANY)
    vmem = pl.BlockSpec(memory_space=pltpu.VMEM)
    dma = pltpu.SemaphoreType.DMA
    new_all, gram, routed = pl.pallas_call(
        functools.partial(encode_kernel, n_mp, n_rows),
        out_shape=(
            jax.ShapeDtypeStruct((n_rows, docs, cols), BF16),
            jax.ShapeDtypeStruct((n_mp, share, anchors), F32),
            jax.ShapeDtypeStruct((n_mp, n_rows, share, cap), BF16),
        ),
        in_specs=[
            vmem, vmem, hbm, hbm, hbm, hbm, vmem, vmem, hbm, hbm, vmem, vmem, vmem, hbm, vmem,
        ],
        out_specs=(hbm, hbm, hbm),
        scratch_shapes=[
            pltpu.VMEM((width, q_width), BF16),
            pltpu.VMEM((width, kv_width), BF16),
            pltpu.VMEM((width, kv_width), BF16),
            pltpu.VMEM((q_width, width), BF16),
            pltpu.VMEM(key_cache.shape, BF16),
            pltpu.VMEM(value_cache.shape, BF16),
            pltpu.VMEM(slab.shape, BF16),
            pltpu.VMEM((docs, width), BF16),
            pltpu.VMEM((docs, q_width), F32),
            pltpu.VMEM((docs, kv_width), F32),
            pltpu.VMEM((docs, kv_width), F32),
            pltpu.VMEM((docs, q_width), BF16),
            pltpu.VMEM((2, mp_half, docs, cols), F32),
            pltpu.VMEM((mp_half, docs, cols), F32),
            pltpu.VMEM((mp_half, docs, cols), F32),
            pltpu.VMEM((far_mp, docs, cols), F32),
            pltpu.VMEM((docs, 128), F32),
            pltpu.VMEM((n_mp - 1, docs, 128), F32),
            pltpu.VMEM((n_rows, docs, cols), BF16),
            pltpu.VMEM((n_rows, docs, cols), BF16),
            pltpu.VMEM((2, mp_half, share, side_width), F32),
            pltpu.VMEM((mp_half, share, side_width), F32),
            pltpu.VMEM((mp_half, share, side_width), F32),
            pltpu.VMEM((far_mp, share, side_width), F32),
            pltpu.VMEM((n_rows, share, cap), BF16),
            pltpu.VMEM((n_mp, n_rows, share, cap), BF16),
            pltpu.VMEM((n_mp, share, anchors), F32),
            dma((3,)), dma((3, CHUNKS)), dma((n_mp,)),
            dma((2, 1)), dma((2, far_mp)), dma((2, n_mp - 1)),
            dma((2, far_rows)), dma((2, rows_half)),
            dma((2, far_rows)), dma((2, rows_half)),
            dma((2, 1)), dma((2, far_mp)),
            dma((2, n_rows - 1)),
            dma((2, far_mp)), dma((2, mp_half)),
            dma((2, far_mp)), dma((2, mp_half)),
            dma((3,)),
        ],
        compiler_params=pltpu.CompilerParams(
            collective_id=0, has_side_effects=True, vmem_limit_bytes=56 * 2**20
        ),
        name="encode",
    )(
        hidden, attn_gain.reshape(1, -1), w_query, w_key, w_value, w_output,
        query_gain.reshape(1, -1), key_gain.reshape(1, -1), key_cache, value_cache,
        lengths.reshape(1, -1), final_gain.reshape(1, -1), old_embed, slab, owners,
    )
    tile = min(256, cols)
    return pl.pallas_call(
        functools.partial(solve_kernel, 0.125 * D),
        out_shape=jax.ShapeDtypeStruct((n_rows * cap, cols), BF16),
        grid=(cols // tile,),
        in_specs=[
            pl.BlockSpec((anchors, tile), lambda i: (0, i)),
            pl.BlockSpec((anchors, anchors), lambda i: (0, 0)),
            pl.BlockSpec((n_mp, n_rows, share, cap), lambda i: (0, 0, 0, 0)),
        ],
        out_specs=pl.BlockSpec((n_rows * cap, tile), lambda i: (0, i)),
        compiler_params=pltpu.CompilerParams(vmem_limit_bytes=48 * 2**20),
        name="solve",
    )(new_all.reshape(anchors, cols), gram.reshape(anchors, anchors), routed)


def solution(mesh):
    return jax.shard_map(
        local,
        mesh=mesh,
        in_specs=(
            P("rows", None),
            P(),
            P(None, "mp"),
            P(None, "mp"),
            P(None, "mp"),
            P("mp", None),
            P(),
            P(),
            P("rows", None, "mp"),
            P("rows", None, "mp"),
            P("rows"),
            P(),
            P("rows", None),
            P("rows", "mp"),
            P("rows", None),
        ),
        out_specs=P("rows", "mp"),
        check_vma=False,
    )
```

time: 634 us -> 52.8 us (0.08)
  waiting for transfers between devices: 376 us -> 0 us
  blocking collectives: 156 us -> 0 us
  Pallas kernels: 0 us -> 48 us
  matrix products: 46.8 us -> 0 us
  other arithmetic: 20.8 us -> 0 us
  between operations: 13.9 us -> 0.02 us
  local copies, waits for them, and re-layouts: 12 us -> 4.56 us
  starting transfers between devices: 6.56 us -> 0 us
    psum x4 -> x0, waiting for transfers between devices: 220 us -> none  [the longest x3 194 us: local(): lax.psum((jnp.dot(old32, direction, precision=highest), jnp.sum(direction...]
    all_gather x2 -> x0, waiting for transfers between devices: 155 us -> none  [the longest x1 126 us: local(): lax.all_gather(map_b, 'rows', axis=0, tiled=True)]
    psum x5 -> x0, blocking collectives: 79.5 us -> none  [the longest x3 51.3 us: column_total(): return lax.psum(jnp.sum(current * current, axis=0), 'rows')]
    all_to_all x1 -> x0, blocking collectives: 50.9 us -> none  [local(): lax.all_to_all(outgoing, 'rows', split_axis=0, concat_axis=0, tiled=True)]
    pallas_call x0 -> x2, Pallas kernels: none -> 48 us  [the longest x1 39.9 us: local(): pl.pallas_call(functools.partial(encode_kernel, n_mp, n_rows), out_shape=...]
    dot_general x14 -> x0, matrix products: 46.8 us -> none  [the longest x3 10.7 us: local(): jnp.dot(old32, direction, precision=highest)]
    all_gather x1 -> x0, blocking collectives: 25.6 us -> none  [local(): lax.all_gather(new_cols, 'rows', axis=0, tiled=True)]
    reduce_sum x11 -> x0, other arithmetic: 12.5 us -> none  [the longest x2 5.33 us: local(): jnp.sum(direction * direction, axis=0)]
  transfers between devices with their start and end apart: 7 -> 0, of which waited for: 6 -> 0; matrix products, arithmetic and copies ran while one was open for 2% -> 0% of each run, Pallas kernels for 0% -> 0%
where the time goes in v1:
time: 52.8 us; the launch traced here: 52.5 us
  Pallas kernels  48 us (91%)
  local copies, waits for them, and re-layouts  4.56 us (9%)
    pallas_call x1, Pallas kernels, local(): pl.pallas_call(functools.partial(encode_kernel, n_mp, n_rows), out_shape=...  39.9 us
    pallas_call x1, Pallas kernels, local(): pl.pallas_call(functools.partial(solve_kernel, 0.125 * D), out_shape=jax....  8.06 us
    unnamed x7, local copies, waits for them, and re-layouts  4.56 us

profile of v1, /device:TPU:1, one launch (start us, length us, event | category | flops | bytes accessed | tf_op | source)
XLA Modules:
  0.0 52.5 jit_solution(1634214413814750610)
XLA Ops:
  0.0 1.5 %copy.16.owners = s32[512,1]{1,0:T(8,128)} copy(s32[512,1]{0,1:T(1,128)} %param.29) | data formatting | bytes 4096 | tf_op args[14]
  1.5 39.9 %encode.1 = (bf16[8,32,1024]{2,1,0:T(8,128)(2,1)}, f32[4,64,256]{2,1,0:T(8,128)}, bf16[4,8,64,128]{3,2,1,0:T(8,128)(2,1)}) custom-call(bf16[32,4096]{1,0:T(8,128)(2,1)} %hidden.1, f32[1,4096]{1,0:T(1,128)} %bitcast.13, bf16[4096,1024]{1,0:T(8,128)(2,1)} %w_query.1, bf16[4096,256]{1,0:T(8,128)(2,1)} %w_key.1, bf16[4096,256]{1,0:T(8,128)(2,1)} %w_value.1, ...), custom_call_target="tpu_custom_call" | custom-call | tf_op jit(solution)/shard_map/encode/pallas_call | solution.py:410
  41.5 0.0 copy-start
  41.5 1.0 %copy-done = bf16[8,32,1024]{2,1,0:T(8,128)(2,1)S(1)} copy-done((bf16[8,32,1024]{2,1,0:T(8,128)(2,1)S(1)}, bf16[8,32,1024]{2,1,0:T(8,128)(2,1)}, u32[]{:S(2)}) %copy-start) | copy-done | bytes 524312
  42.5 0.0 copy-start.1
  42.5 1.0 %copy-done.1 = bf16[4,8,64,128]{3,2,1,0:T(8,128)(2,1)S(1)} copy-done((bf16[4,8,64,128]{3,2,1,0:T(8,128)(2,1)S(1)}, bf16[4,8,64,128]{3,2,1,0:T(8,128)(2,1)}, u32[]{:S(2)}) %copy-start.1) | copy-done | bytes 524312
  43.5 0.0 copy-start.2
  43.5 0.9 %copy-done.2 = f32[4,64,256]{2,1,0:T(8,128)S(1)} copy-done((f32[4,64,256]{2,1,0:T(8,128)S(1)}, f32[4,64,256]{2,1,0:T(8,128)}, u32[]{:S(2)}) %copy-start.2) | copy-done | bytes 262168
  44.5 8.1 %solve.1 = bf16[1024,1024]{1,0:T(8,128)(2,1)} custom-call(bf16[256,1024]{1,0:T(8,128)(2,1)S(1)} %bitcast.9, f32[256,256]{1,0:T(8,128)S(1)} %bitcast.10, bf16[4,8,64,128]{3,2,1,0:T(8,128)(2,1)S(1)} %copy-done.1), custom_call_target="tpu_custom_call" | custom-call | tf_op jit(solution)/shard_map/solve/pallas_call | solution.py:469
Async XLA Ops:
  41.5 1.0 %copy-start = (bf16[8,32,1024]{2,1,0:T(8,128)(2,1)S(1)}, bf16[8,32,1024]{2,1,0:T(8,128)(2,1)}, u32[]{:S(2)}) copy-start(bf16[8,32,1024]{2,1,0:T(8,128)(2,1)} %get-tuple-element.8) | copy-start | bytes 1572868
  42.5 1.0 %copy-start.1 = (bf16[4,8,64,128]{3,2,1,0:T(8,128)(2,1)S(1)}, bf16[4,8,64,128]{3,2,1,0:T(8,128)(2,1)}, u32[]{:S(2)}) copy-start(bf16[4,8,64,128]{3,2,1,0:T(8,128)(2,1)} %get-tuple-element.10.routed) | copy-start | bytes 1572868
  43.5 0.9 %copy-start.2 = (f32[4,64,256]{2,1,0:T(8,128)S(1)}, f32[4,64,256]{2,1,0:T(8,128)}, u32[]{:S(2)}) copy-start(f32[4,64,256]{2,1,0:T(8,128)} %get-tuple-element.9) | copy-start | bytes 786436

commit v2 on v1

v2 whole, which is shorter than its diff:
```python
import functools
import math

import jax
import jax.numpy as jnp
from jax import lax
from jax.experimental import pallas as pl
from jax.experimental.pallas import tpu as pltpu
from jax.sharding import PartitionSpec as P

D = 4096
HEADS = 32
KV_HEADS = 8
HEAD = 128
ITERS = 3
MESH = pl.DeviceIdType.MESH
F32 = jnp.float32
BF16 = jnp.bfloat16
CHUNKS = 8


def dot(left, right, left_dim=1, right_dim=0):
    return lax.dot_general(
        left, right, (((left_dim,), (right_dim,)), ((), ())), preferred_element_type=F32
    )


def solve(ridge, start, gram):
    high = gram.astype(BF16)
    low = (gram - high.astype(F32)).astype(BF16)

    def apply(values):
        top = values.astype(BF16)
        rest = (values - top.astype(F32)).astype(BF16)
        return dot(high, top) + (dot(high, rest) + dot(low, top))

    def total(values):
        return jnp.sum(values, axis=0, keepdims=True)

    residual = start
    direction = residual
    image_docs = apply(start)
    res_sq = total(residual * image_docs)
    coeffs = jnp.zeros_like(residual)
    for sweep in range(ITERS):
        curvature = total(image_docs * image_docs) + ridge * total(direction * image_docs)
        alpha = res_sq / curvature
        coeffs = coeffs + alpha * direction
        if sweep + 1 < ITERS:
            residual = residual - alpha * (image_docs + ridge * direction)
            spread = apply(residual)
            new_sq = total(residual * spread)
            ratio = new_sq / res_sq
            direction = residual + ratio * direction
            image_docs = spread + ratio * image_docs
            res_sq = new_sq
    return coeffs


def encode_kernel(
    n_mp, n_rows,
    hidden, attn_gain, w_query, w_key, w_value, w_output, query_gain, key_gain,
    key_cache, value_cache, lengths, final_gain, old_embed, slab, owners,
    out,
    wq, wk, wv, wo, kc, vc, sl, normed, q_acc, k_acc, v_acc, attended,
    part, part_in, part_sum, part_far, sq_own, sq_in, scale_all, new_all,
    old_all, side, side_in, side_sum, side_far, pair, pair_in, pair_sum, pair_far,
    outgoing, routed, gram, staged,
    load_sem, weight_sem, wo_sem,
    part_a, part_b, sq_sem, scale_sem, new_f, new_n, old_f, old_n,
    side_a, side_b, pair_a, pair_b,
    trip_sem, gram_f, gram_n, routed_f, routed_n, out_sem,
):
    mp = lax.axis_index("mp")
    row = lax.axis_index("rows")
    docs, width = hidden.shape
    cols = width // n_mp
    anchors = n_rows * docs
    share = anchors // n_mp
    slab_rows = slab.shape[0]
    cap = outgoing.shape[2]
    chunks, tile = new_all.shape[0], new_all.shape[3]
    kv_local = k_acc.shape[1] // HEAD
    group = HEADS // KV_HEADS
    ctx = key_cache.shape[0] // docs
    mp_half, rows_half = n_mp // 2, n_rows // 2
    mp_slow, core = mp // 2, mp % 2
    row_slow, row_fast = row // 2, row % 2

    def remote(src, dst, sems, spot, to_mp, to_row):
        spot = spot if isinstance(spot, tuple) else (spot,)
        return pltpu.make_async_remote_copy(
            src_ref=src, dst_ref=dst, send_sem=sems.at[(0, *spot)],
            recv_sem=sems.at[(1, *spot)],
            device_id={"mp": to_mp, "rows": to_row}, device_id_type=MESH,
        )

    def far_rows(buf, sems, *lead):
        return [
            remote(buf.at[(*lead, row)], buf.at[(*lead, row)], sems, (*lead, off - 1), mp,
                   ((row_slow + off) % rows_half) * 2 + row_fast)
            for off in range(1, rows_half)
        ]

    def near_rows(buf, sems, *lead):
        found = []
        for off in range(rows_half):
            block = ((row_slow + rows_half - off) % rows_half) * 2 + row_fast
            found.append(remote(buf.at[(*lead, block)], buf.at[(*lead, block)], sems,
                                (*lead, off), mp, row_slow * 2 + 1 - row_fast))
        return found

    def far_mp(buf, sems):
        return [
            remote(buf.at[mp], buf.at[mp], sems, off - 1,
                   ((mp_slow + off) % mp_half) * 2 + core, row)
            for off in range(1, mp_half)
        ]

    def near_mp(buf, sems):
        found = []
        for off in range(mp_half):
            block = ((mp_slow + mp_half - off) % mp_half) * 2 + core
            found.append(remote(buf.at[block], buf.at[block], sems, off,
                                mp_slow * 2 + 1 - core, row))
        return found

    def reduce_near(partial, landed, sems, *lead):
        return remote(partial.at[(*lead, 1 - core)], landed.at[lead] if lead else landed, sems,
                      (*lead, 0), mp_slow * 2 + 1 - core, row)

    def reduce_far(summed, landed, sems, *lead):
        found = []
        for off in range(1, mp_half):
            there = (mp_slow + off) % mp_half
            found.append(remote(summed.at[(*lead, there)], landed.at[(*lead, off - 1)], sems,
                                (*lead, off - 1), there * 2 + core, row))
        return found

    def start(copies):
        for copy in copies:
            copy.start()

    sent = []

    def received(copies):
        for copy in copies:
            copy.wait_recv()
            sent.append(copy)

    depth = width // CHUNKS

    def weight_copies(step):
        span = pl.ds(pl.multiple_of(step * depth, depth), depth)
        return [
            pltpu.make_async_copy(src.at[span, :], dst.at[span, :], weight_sem.at[i, step])
            for i, (src, dst) in enumerate(((w_query, wq), (w_key, wk), (w_value, wv)))
        ]

    def output_block(step):
        step = step % n_mp
        return 2 * (step % mp_half) + lax.rem(core + 1 + step // mp_half, 2)

    def output_span(step):
        base = output_block(step) * cols + step // n_mp * tile
        return pl.ds(pl.multiple_of(base, tile), tile)

    def output_copy(step):
        span = output_span(step)
        return pltpu.make_async_copy(w_output.at[:, span], wo.at[:, span], wo_sem.at[step])

    for step in range(CHUNKS):
        start(weight_copies(step))
    loads = [
        pltpu.make_async_copy(key_cache, kc, load_sem.at[0]),
        pltpu.make_async_copy(value_cache, vc, load_sem.at[1]),
        pltpu.make_async_copy(slab, sl, load_sem.at[2]),
    ]
    start(loads)
    for step in range(n_mp * chunks):
        output_copy(step).start()

    barrier = pltpu.get_barrier_semaphore()
    for off in range(1, n_rows):
        pl.semaphore_signal(barrier, inc=1, device_id={"mp": mp, "rows": lax.rem(row + off, n_rows)},
                            device_id_type=MESH)
    for off in range(1, n_mp):
        pl.semaphore_signal(barrier, inc=1, device_id={"mp": lax.rem(mp + off, n_mp), "rows": row},
                            device_id_type=MESH)
    mine = pl.ds(pl.multiple_of(mp * cols, cols), cols)
    old_all[row] = old_embed[:, mine]
    pl.semaphore_wait(barrier, n_rows + n_mp - 2)

    old_far = far_rows(old_all, old_f)
    start(old_far)
    old_near = near_rows(old_all, old_n)
    old_near[0].start()

    hidden32 = hidden[...].astype(F32)
    normed[...] = (
        hidden32 * lax.rsqrt(jnp.mean(hidden32 * hidden32, axis=-1, keepdims=True) + 1e-06)
        * attn_gain[...]
    ).astype(BF16)

    q_acc[...] = jnp.zeros_like(q_acc)
    k_acc[...] = jnp.zeros_like(k_acc)
    v_acc[...] = jnp.zeros_like(v_acc)

    def project(step, carry):
        span = pl.ds(pl.multiple_of(step * depth, depth), depth)
        for copy in weight_copies(step):
            copy.wait()
        piece = normed[:, span]
        q_acc[...] += dot(piece, wq[span, :])
        k_acc[...] += dot(piece, wk[span, :])
        v_acc[...] += dot(piece, wv[span, :])
        return carry

    lax.fori_loop(0, CHUNKS, project, 0)

    received(old_far)
    start(old_near[1:])

    tall = group * docs
    spot = lax.broadcasted_iota(jnp.int32, (tall, docs), 0) % docs
    named = lax.broadcasted_iota(jnp.int32, (tall, docs), 1)
    length = jnp.sum(
        jnp.where(spot == named, lengths[...].astype(F32), 0.0), axis=-1, keepdims=True
    )
    lane = lax.broadcasted_iota(jnp.int32, (docs, HEAD), 1)
    half = HEAD // 2
    frequency = jnp.exp(
        -(2.0 * (lane % half).astype(F32) / HEAD) * math.log(1000000.0)
    )
    angle = length[:docs] * frequency
    cosine = jnp.cos(angle)
    sine = jnp.sin(angle) * jnp.where(lane < half, -1.0, 1.0)

    def turned(values, gain):
        scale = lax.rsqrt(jnp.mean(values * values, axis=-1, keepdims=True) + 1e-06)
        values = values * scale * gain
        return (values * cosine + pltpu.roll(values, half, 1) * sine).astype(BF16)

    loads[0].wait()
    loads[1].wait()
    place_row = lax.broadcasted_iota(jnp.int32, (tall, docs * ctx), 0) % docs * ctx
    place_lane = lax.broadcasted_iota(jnp.int32, (tall, docs * ctx), 1)
    valid = (place_lane >= place_row) & (place_lane < place_row + length.astype(jnp.int32))
    for g in range(kv_local):
        span = slice(g * HEAD, (g + 1) * HEAD)
        queries = jnp.concatenate(
            [
                turned(q_acc[:, (g * group + h) * HEAD:(g * group + h + 1) * HEAD], query_gain[...])
                for h in range(group)
            ],
            axis=0,
        )
        key_new = jnp.concatenate([turned(k_acc[:, span], key_gain[...])] * group, axis=0)
        value_new = jnp.concatenate([v_acc[:, span].astype(BF16)] * group, axis=0)
        factor = 1.0 / math.sqrt(HEAD)
        scores = jnp.where(valid, dot(queries, kc[:, span], 1, 1) * factor, -jnp.inf)
        own_score = jnp.sum(
            queries.astype(F32) * key_new.astype(F32), axis=-1, keepdims=True
        ) * factor
        top = jnp.maximum(jnp.max(scores, axis=-1, keepdims=True), own_score)
        expo = jnp.exp(scores - top)
        own_expo = jnp.exp(own_score - top)
        inverse = 1.0 / (jnp.sum(expo, axis=-1, keepdims=True) + own_expo)
        weights = (expo * inverse).astype(BF16)
        own_weight = (own_expo * inverse).astype(BF16).astype(F32)
        mixed = dot(weights, vc[:, span]) + own_weight * value_new.astype(F32)
        for h in range(group):
            attended[:, (g * group + h) * HEAD:(g * group + h + 1) * HEAD] = mixed[
                h * docs:(h + 1) * docs
            ].astype(BF16)

    def project_out(chunk, first):
        for step in range(first, first + mp_half):
            step = chunk * n_mp + step
            output_copy(step).wait()
            block = output_block(step)
            part[chunk, block % 2, block // 2] = dot(attended[...], wo[:, output_span(step)])

    part_near = [reduce_near(part, part_in, part_a, c) for c in range(chunks)]
    part_apart = [reduce_far(part_sum, part_far, part_b, c) for c in range(chunks)]

    def add_near(c):
        received([part_near[c]])
        part_sum[c] = part[c, core] + part_in[c]
        start(part_apart[c])

    for c in range(chunks):
        project_out(c, 0)
        part_near[c].start()
        project_out(c, mp_half)
        if c:
            add_near(c - 1)

    received(old_near)
    loads[2].wait()
    olds = old_all[...].reshape(anchors, cols)
    product = dot(olds, sl[...], 1, 1)
    for j in range(n_mp):
        side[j % 2, j // 2] = product[j * share:(j + 1) * share]
    side_near = reduce_near(side, side_in, side_a)
    side_near.start()
    add_near(chunks - 1)
    product = dot(olds, olds, 1, 1)
    for j in range(n_mp):
        pair[j % 2, j // 2] = product[j * share:(j + 1) * share]
    pair_near = reduce_near(pair, pair_in, pair_a)
    pair_near.start()

    new_far = [far_rows(new_all, new_f, c) for c in range(chunks)]
    new_near = [near_rows(new_all, new_n, c) for c in range(chunks)]
    square = jnp.zeros((docs, 1), F32)
    for c in range(chunks):
        received(part_apart[c])
        span = pl.ds(pl.multiple_of(mp * cols + c * tile, tile), tile)
        state = hidden[:, span].astype(F32) + part_sum[c, mp_slow]
        for off in range(1, mp_half):
            state = state + part_far[c, off - 1]
        new_all[c, row] = (state * final_gain[:, span]).astype(BF16)
        start(new_far[c])
        new_near[c][0].start()
        square = square + jnp.sum(state * state, axis=-1, keepdims=True)
    sq_own[...] = jnp.broadcast_to(square, sq_own.shape)
    sq_copies = [
        remote(sq_own, sq_in.at[off - 1], sq_sem, off - 1, lax.rem(mp + off, n_mp), row)
        for off in range(1, n_mp)
    ]
    start(sq_copies)

    received([side_near])
    side_sum[...] = side[core] + side_in[...]
    side_apart = reduce_far(side_sum, side_far, side_b)
    start(side_apart)
    received([pair_near])
    pair_sum[...] = pair[core] + pair_in[...]
    pair_apart = reduce_far(pair_sum, pair_far, pair_b)
    start(pair_apart)

    owner = owners[...]
    chosen = jnp.where(
        owner == lax.broadcasted_iota(jnp.int32, (n_rows, slab_rows), 0), 1.0, 0.0
    )
    earlier = jnp.where(
        lax.broadcasted_iota(jnp.int32, (slab_rows, slab_rows), 0)
        < lax.broadcasted_iota(jnp.int32, (slab_rows, slab_rows), 1), 1.0, 0.0
    )
    slot = jnp.sum(
        dot(chosen.astype(BF16), earlier.astype(BF16)) * chosen, axis=0, keepdims=True
    )
    target = owner.astype(F32) * cap + slot

    received(sq_copies)
    total = sq_own[...]
    for off in range(1, n_mp):
        total = total + sq_in[off - 1]
    scale_all[row] = lax.rsqrt(total / width + 1e-06)
    scale_copies = [
        remote(scale_all.at[row], scale_all.at[row], scale_sem, off - 1, mp,
               lax.rem(row + off, n_rows))
        for off in range(1, n_rows)
    ]
    start(scale_copies)

    def forward(c):
        received(new_far[c])
        start(new_near[c][1:])

    for c in range(chunks // 2):
        forward(c)

    received(side_apart)
    whole = side_sum[mp_slow]
    for off in range(1, mp_half):
        whole = whole + side_far[off - 1]
    body = whole.astype(BF16)
    seats = lax.broadcasted_iota(jnp.int32, (cap, slab_rows), 0).astype(F32)
    for o in range(n_rows):
        put = jnp.where(target == seats + float(o * cap), 1.0, 0.0).astype(BF16)
        outgoing[o] = dot(body, put, 1, 1).astype(BF16)
    trips = []
    for off in range(1, n_rows):
        there = lax.rem(row + off, n_rows)
        trips.append(remote(outgoing.at[there], routed.at[mp, row], trip_sem, off - 1, mp, there))
    start(trips)
    routed[mp, row] = outgoing[row]

    received(pair_apart)
    whole = pair_sum[mp_slow]
    for off in range(1, mp_half):
        whole = whole + pair_far[off - 1]
    gram[mp] = whole
    gram_far = far_mp(gram, gram_f)
    start(gram_far)
    gram_near = near_mp(gram, gram_n)
    gram_near[0].start()

    for c in range(chunks // 2, chunks):
        forward(c)

    received(trips)
    routed_far = far_mp(routed, routed_f)
    start(routed_far)
    routed_near = near_mp(routed, routed_n)
    routed_near[0].start()
    received(gram_far)
    start(gram_near[1:])
    received(routed_far)
    start(routed_near[1:])

    received(gram_near)
    received(scale_copies)
    scale = scale_all[...].reshape(anchors, HEAD)[:, :1]
    outs = []
    for c in range(chunks):
        received(new_near[c])
        targets = new_all[c].reshape(anchors, tile).astype(F32) * scale
        coeffs = solve(0.125 * D, targets, gram[...].reshape(anchors, anchors))
        top = coeffs.astype(BF16)
        rest = (coeffs - top.astype(F32)).astype(BF16)
        if c == 0:
            received(routed_near)
        for b in range(n_rows):
            block = routed[:, b].reshape(anchors, cap)
            staged[c, b * cap:(b + 1) * cap] = (
                dot(block, top, 0, 0) + dot(block, rest, 0, 0)
            ).astype(BF16)
        outs.append(
            pltpu.make_async_copy(
                staged.at[c], out.at[:, c * tile:(c + 1) * tile], out_sem.at[c]
            )
        )
        outs[c].start()
    for copy in sent:
        copy.wait_send()
    for copy in outs:
        copy.wait()


def local(
    hidden, attn_gain, w_query, w_key, w_value, w_output, query_gain, key_gain,
    key_cache, value_cache, lengths, final_gain, old_embed, slab, owners,
):
    n_rows = lax.axis_size("rows")
    n_mp = lax.axis_size("mp")
    docs, width = hidden.shape
    cols = width // n_mp
    anchors = n_rows * docs
    share = anchors // n_mp
    slab_rows = slab.shape[0]
    cap = 2 * slab_rows // n_rows
    kv_width = w_key.shape[1]
    q_width = w_query.shape[1]
    mp_half, rows_half = n_mp // 2, n_rows // 2
    key_cache = key_cache.reshape(-1, kv_width)
    value_cache = value_cache.reshape(-1, kv_width)
    tile = min(256, cols)
    chunks = cols // tile
    far_mp, far_rows = max(mp_half - 1, 1), max(rows_half - 1, 1)
    hbm = pl.BlockSpec(memory_space=pl.ANY)
    vmem = pl.BlockSpec(memory_space=pltpu.VMEM)
    dma = pltpu.SemaphoreType.DMA
    return pl.pallas_call(
        functools.partial(encode_kernel, n_mp, n_rows),
        out_shape=jax.ShapeDtypeStruct((n_rows * cap, cols), BF16),
        in_specs=[
            vmem, vmem, hbm, hbm, hbm, hbm, vmem, vmem, hbm, hbm, vmem, vmem, vmem, hbm, vmem,
        ],
        out_specs=hbm,
        scratch_shapes=[
            pltpu.VMEM((width, q_width), BF16),
            pltpu.VMEM((width, kv_width), BF16),
            pltpu.VMEM((width, kv_width), BF16),
            pltpu.VMEM((q_width, width), BF16),
            pltpu.VMEM(key_cache.shape, BF16),
            pltpu.VMEM(value_cache.shape, BF16),
            pltpu.VMEM(slab.shape, BF16),
            pltpu.VMEM((docs, width), BF16),
            pltpu.VMEM((docs, q_width), F32),
            pltpu.VMEM((docs, kv_width), F32),
            pltpu.VMEM((docs, kv_width), F32),
            pltpu.VMEM((docs, q_width), BF16),
            pltpu.VMEM((chunks, 2, mp_half, docs, tile), F32),
            pltpu.VMEM((chunks, mp_half, docs, tile), F32),
            pltpu.VMEM((chunks, mp_half, docs, tile), F32),
            pltpu.VMEM((chunks, far_mp, docs, tile), F32),
            pltpu.VMEM((docs, 128), F32),
            pltpu.VMEM((n_mp - 1, docs, 128), F32),
            pltpu.VMEM((n_rows, docs, 128), F32),
            pltpu.VMEM((chunks, n_rows, docs, tile), BF16),
            pltpu.VMEM((n_rows, docs, cols), BF16),
            pltpu.VMEM((2, mp_half, share, slab_rows), F32),
            pltpu.VMEM((mp_half, share, slab_rows), F32),
            pltpu.VMEM((mp_half, share, slab_rows), F32),
            pltpu.VMEM((far_mp, share, slab_rows), F32),
            pltpu.VMEM((2, mp_half, share, anchors), F32),
            pltpu.VMEM((mp_half, share, anchors), F32),
            pltpu.VMEM((mp_half, share, anchors), F32),
            pltpu.VMEM((far_mp, share, anchors), F32),
            pltpu.VMEM((n_rows, share, cap), BF16),
            pltpu.VMEM((n_mp, n_rows, share, cap), BF16),
            pltpu.VMEM((n_mp, share, anchors), F32),
            pltpu.VMEM((chunks, n_rows * cap, tile), BF16),
            dma((3,)), dma((3, CHUNKS)), dma((n_mp * chunks,)),
            dma((2, chunks, 1)), dma((2, chunks, far_mp)), dma((2, n_mp - 1)),
            dma((2, n_rows - 1)),
            dma((2, chunks, far_rows)), dma((2, chunks, rows_half)),
            dma((2, far_rows)), dma((2, rows_half)),
            dma((2, 1)), dma((2, far_mp)),
            dma((2, 1)), dma((2, far_mp)),
            dma((2, n_rows - 1)),
            dma((2, far_mp)), dma((2, mp_half)),
            dma((2, far_mp)), dma((2, mp_half)),
            dma((chunks,)),
        ],
        compiler_params=pltpu.CompilerParams(
            collective_id=0, has_side_effects=True, vmem_limit_bytes=56 * 2**20
        ),
        name="encode",
    )(
        hidden, attn_gain.reshape(1, -1), w_query, w_key, w_value, w_output,
        query_gain.reshape(1, -1), key_gain.reshape(1, -1), key_cache, value_cache,
        lengths.reshape(1, -1), final_gain.reshape(1, -1), old_embed, slab, owners.reshape(1, -1),
    )

def solution(mesh):
    return jax.shard_map(
        local,
        mesh=mesh,
        in_specs=(
            P("rows", None),
            P(),
            P(None, "mp"),
            P(None, "mp"),
            P(None, "mp"),
            P("mp", None),
            P(),
            P(),
            P("rows", None, "mp"),
            P("rows", None, "mp"),
            P("rows"),
            P(),
            P("rows", None),
            P("rows", "mp"),
            P("rows", None),
        ),
        out_specs=P("rows", "mp"),
        check_vma=False,
    )
```

time: 52.8 us -> 51.6 us (0.977)
  local copies, waits for them, and re-layouts: 4.56 us -> 3.08 us
    pallas_call x1 -> x0, Pallas kernels: 8.06 us -> none  [local(): pl.pallas_call(functools.partial(solve_kernel, 0.125 * D), out_shape=jax....]
    pallas_call x1, Pallas kernels: 39.9 us -> 47.8 us  [local(): pl.pallas_call(functools.partial(encode_kernel, n_mp, n_rows), out_shape=...]
    unnamed x7 -> x1, local copies, waits for them, and re-layouts: 4.56 us -> 3.08 us
where the time goes in v2:
time: 51.6 us; the launch traced here: 50.8 us
  Pallas kernels  47.8 us (93%)
  local copies, waits for them, and re-layouts  3.08 us (6%)
    pallas_call x1, Pallas kernels, local(): pl.pallas_call(functools.partial(encode_kernel, n_mp, n_rows), out_shape=...  47.8 us
    unnamed x1, local copies, waits for them, and re-layouts  3.08 us

profile of v2, /device:TPU:1, one launch (start us, length us, event | category | flops | bytes accessed | tf_op | source)
XLA Modules:
  0.0 50.8 jit_solution(1708648604412254176)
XLA Ops:
  0.0 47.8 %encode.1 = bf16[1024,1024]{1,0:T(8,128)(2,1)} custom-call(bf16[32,4096]{1,0:T(8,128)(2,1)} %hidden.1, f32[1,4096]{1,0:T(1,128)} %bitcast.10, bf16[4096,1024]{1,0:T(8,128)(2,1)} %w_query.1, bf16[4096,256]{1,0:T(8,128)(2,1)} %w_key.1, bf16[4096,256]{1,0:T(8,128)(2,1)} %w_value.1, bf16[1024,4096]{1,0:T(8,128)(2,1)} %w_output.1, f32[1,128]{1,0:T(1,128)} %bitcast.13, ...), custom_call_target="tpu_custom_call" | custom-call | tf_op jit(solution)/shard_map/encode/pallas_call | solution.py:466
  47.8 3.1 %copy.17 = bf16[1024,1024]{1,0:T(8,128)(2,1)} copy(bf16[1024,1024]{1,0:T(8,128)(2,1)} %encode.1) | data formatting | bytes 4194304

commit v3 on v2

--- a/solution.py
+++ b/solution.py
@@ -59,13 +59,14 @@
 
 def encode_kernel(
     n_mp, n_rows,
-    hidden, attn_gain, w_query, w_key, w_value, w_output, query_gain, key_gain,
-    key_cache, value_cache, lengths, final_gain, old_embed, slab, owners,
+    hidden_in, attn_gain_in, w_query, w_key, w_value, w_output, query_gain_in, key_gain_in,
+    key_cache, value_cache, lengths_in, final_gain_in, old_embed, slab, owners_in,
     out,
+    hidden, attn_gain, query_gain, key_gain, lengths, final_gain, owners,
     wq, wk, wv, wo, kc, vc, sl, normed, q_acc, k_acc, v_acc, attended,
     part, part_in, part_sum, part_far, sq_own, sq_in, scale_all, new_all,
     old_all, side, side_in, side_sum, side_far, pair, pair_in, pair_sum, pair_far,
-    outgoing, routed, gram, staged,
+    outgoing, routed, gram, spread_length, spread_scale, mapped, rows_t, puts, staged,
     load_sem, weight_sem, wo_sem,
     part_a, part_b, sq_sem, scale_sem, new_f, new_n, old_f, old_n,
     side_a, side_b, pair_a, pair_b,
@@ -169,17 +170,6 @@
         span = output_span(step)
         return pltpu.make_async_copy(w_output.at[:, span], wo.at[:, span], wo_sem.at[step])
 
-    for step in range(CHUNKS):
-        start(weight_copies(step))
-    loads = [
-        pltpu.make_async_copy(key_cache, kc, load_sem.at[0]),
-        pltpu.make_async_copy(value_cache, vc, load_sem.at[1]),
-        pltpu.make_async_copy(slab, sl, load_sem.at[2]),
-    ]
-    start(loads)
-    for step in range(n_mp * chunks):
-        output_copy(step).start()
-
     barrier = pltpu.get_barrier_semaphore()
     for off in range(1, n_rows):
         pl.semaphore_signal(barrier, inc=1, device_id={"mp": mp, "rows": lax.rem(row + off, n_rows)},
@@ -188,23 +178,65 @@
         pl.semaphore_signal(barrier, inc=1, device_id={"mp": lax.rem(mp + off, n_mp), "rows": row},
                             device_id_type=MESH)
     mine = pl.ds(pl.multiple_of(mp * cols, cols), cols)
-    old_all[row] = old_embed[:, mine]
-    pl.semaphore_wait(barrier, n_rows + n_mp - 2)
-
-    old_far = far_rows(old_all, old_f)
-    start(old_far)
-    old_near = near_rows(old_all, old_n)
-    old_near[0].start()
-
+    loads = [
+        pltpu.make_async_copy(src, dst, load_sem.at[i])
+        for i, (src, dst) in enumerate((
+            (key_cache, kc), (value_cache, vc), (slab, sl),
+            (hidden_in, hidden), (attn_gain_in, attn_gain),
+            (old_embed.at[:, mine], old_all.at[row]), (owners_in, owners),
+            (lengths_in, lengths), (query_gain_in, query_gain), (key_gain_in, key_gain),
+            (final_gain_in, final_gain),
+        ))
+    ]
+    start(loads[3:])
+    for step in range(CHUNKS):
+        start(weight_copies(step))
+    start(loads[:3])
+    for step in range(n_mp * chunks):
+        output_copy(step).start()
+
+    loads[3].wait()
+    loads[4].wait()
     hidden32 = hidden[...].astype(F32)
     normed[...] = (
         hidden32 * lax.rsqrt(jnp.mean(hidden32 * hidden32, axis=-1, keepdims=True) + 1e-06)
         * attn_gain[...]
     ).astype(BF16)
+    for copy in loads[5:]:
+        copy.wait()
+    pl.semaphore_wait(barrier, n_rows + n_mp - 2)
+
+    old_far = far_rows(old_all, old_f)
+    start(old_far)
+    old_near = near_rows(old_all, old_n)
+    old_near[0].start()
 
     q_acc[...] = jnp.zeros_like(q_acc)
     k_acc[...] = jnp.zeros_like(k_acc)
     v_acc[...] = jnp.zeros_like(v_acc)
+
+    owner = owners[...]
+    chosen = jnp.where(
+        owner == lax.broadcasted_iota(jnp.int32, (n_rows, slab_rows), 0), 1.0, 0.0
+    )
+    earlier = jnp.where(
+        lax.broadcasted_iota(jnp.int32, (slab_rows, slab_rows), 0)
+        < lax.broadcasted_iota(jnp.int32, (slab_rows, slab_rows), 1), 1.0, 0.0
+    )
+    slot = jnp.sum(
+        dot(chosen.astype(BF16), earlier.astype(BF16)) * chosen, axis=0, keepdims=True
+    )
+    target = owner.astype(F32) * cap + slot
+    seats = lax.broadcasted_iota(jnp.int32, (cap, slab_rows), 0).astype(F32)
+
+    def put(o, carry):
+        base = (o * cap).astype(F32)
+        puts[pl.ds(pl.multiple_of(o * cap, cap), cap)] = jnp.where(
+            target - base == seats, 1.0, 0.0
+        ).astype(BF16)
+        return carry
+
+    lax.fori_loop(0, n_rows, put, 0)
 
     def project(step, carry):
         span = pl.ds(pl.multiple_of(step * depth, depth), depth)
@@ -216,14 +248,17 @@
         v_acc[...] += dot(piece, wv[span, :])
         return carry
 
-    lax.fori_loop(0, CHUNKS, project, 0)
-
-    received(old_far)
-    start(old_near[1:])
-
-    tall = group * docs
-    spot = lax.broadcasted_iota(jnp.int32, (tall, docs), 0) % docs
-    named = lax.broadcasted_iota(jnp.int32, (tall, docs), 1)
+    done = CHUNKS // 2
+    lax.fori_loop(0, done, project, 0)
+    for off in range(1, rows_half):
+        lax.fori_loop(done, max(done, CHUNKS * (rows_half + off) // (2 * rows_half)), project, 0)
+        done = max(done, CHUNKS * (rows_half + off) // (2 * rows_half))
+        received(old_far[off - 1:off])
+        old_near[off].start()
+    lax.fori_loop(done, CHUNKS, project, 0)
+
+    spot = lax.broadcasted_iota(jnp.int32, (docs, docs), 0)
+    named = lax.broadcasted_iota(jnp.int32, (docs, docs), 1)
     length = jnp.sum(
         jnp.where(spot == named, lengths[...].astype(F32), 0.0), axis=-1, keepdims=True
     )
@@ -232,83 +267,116 @@
     frequency = jnp.exp(
         -(2.0 * (lane % half).astype(F32) / HEAD) * math.log(1000000.0)
     )
-    angle = length[:docs] * frequency
+    angle = length * frequency
     cosine = jnp.cos(angle)
     sine = jnp.sin(angle) * jnp.where(lane < half, -1.0, 1.0)
 
     def turned(values, gain):
         scale = lax.rsqrt(jnp.mean(values * values, axis=-1, keepdims=True) + 1e-06)
         values = values * scale * gain
-        return (values * cosine + pltpu.roll(values, half, 1) * sine).astype(BF16)
+        return values * cosine + pltpu.roll(values, half, 1) * sine
 
     loads[0].wait()
     loads[1].wait()
-    place_row = lax.broadcasted_iota(jnp.int32, (tall, docs * ctx), 0) % docs * ctx
-    place_lane = lax.broadcasted_iota(jnp.int32, (tall, docs * ctx), 1)
-    valid = (place_lane >= place_row) & (place_lane < place_row + length.astype(jnp.int32))
+    few = min(8, docs)
+    tall, wide = group * few, few * ctx
+    place_row = lax.broadcasted_iota(jnp.int32, (tall, wide), 0) % few * ctx
+    place_lane = lax.broadcasted_iota(jnp.int32, (tall, wide), 1)
+    factor = 1.0 / math.sqrt(HEAD)
+    spread_length[...] = jnp.broadcast_to(length, spread_length.shape)
+
+    def turn_query(h, carry):
+        span = pl.ds(pl.multiple_of(h * HEAD, HEAD), HEAD)
+        q_acc[:, span] = turned(q_acc[:, span], query_gain[...])
+        return carry
+
+    lax.fori_loop(0, kv_local * group, turn_query, 0)
     for g in range(kv_local):
         span = slice(g * HEAD, (g + 1) * HEAD)
-        queries = jnp.concatenate(
-            [
-                turned(q_acc[:, (g * group + h) * HEAD:(g * group + h + 1) * HEAD], query_gain[...])
-                for h in range(group)
-            ],
-            axis=0,
-        )
-        key_new = jnp.concatenate([turned(k_acc[:, span], key_gain[...])] * group, axis=0)
-        value_new = jnp.concatenate([v_acc[:, span].astype(BF16)] * group, axis=0)
-        factor = 1.0 / math.sqrt(HEAD)
-        scores = jnp.where(valid, dot(queries, kc[:, span], 1, 1) * factor, -jnp.inf)
-        own_score = jnp.sum(
-            queries.astype(F32) * key_new.astype(F32), axis=-1, keepdims=True
-        ) * factor
-        top = jnp.maximum(jnp.max(scores, axis=-1, keepdims=True), own_score)
-        expo = jnp.exp(scores - top)
-        own_expo = jnp.exp(own_score - top)
-        inverse = 1.0 / (jnp.sum(expo, axis=-1, keepdims=True) + own_expo)
-        weights = (expo * inverse).astype(BF16)
-        own_weight = (own_expo * inverse).astype(BF16).astype(F32)
-        mixed = dot(weights, vc[:, span]) + own_weight * value_new.astype(F32)
-        for h in range(group):
-            attended[:, (g * group + h) * HEAD:(g * group + h + 1) * HEAD] = mixed[
-                h * docs:(h + 1) * docs
-            ].astype(BF16)
-
-    def project_out(chunk, first):
-        for step in range(first, first + mp_half):
-            step = chunk * n_mp + step
-            output_copy(step).wait()
-            block = output_block(step)
-            part[chunk, block % 2, block // 2] = dot(attended[...], wo[:, output_span(step)])
+        k_acc[:, span] = turned(k_acc[:, span], key_gain[...]).astype(BF16).astype(F32)
+    v_acc[...] = v_acc[...].astype(BF16).astype(F32)
+
+    def attend(block, carry):
+        some = pl.ds(pl.multiple_of(block * few, few), few)
+        held = pl.ds(pl.multiple_of(block * few * ctx, few * ctx), few * ctx)
+        long = jnp.concatenate([spread_length[some, :1]] * group, axis=0).astype(jnp.int32)
+        valid = (place_lane >= place_row) & (place_lane < place_row + long)
+        for g in range(kv_local):
+            span = slice(g * HEAD, (g + 1) * HEAD)
+            heads = [
+                slice((g * group + h) * HEAD, (g * group + h + 1) * HEAD) for h in range(group)
+            ]
+            ask = jnp.concatenate([q_acc[some, head] for head in heads], axis=0).astype(BF16)
+            scores = jnp.where(valid, dot(ask, kc[held, span], 1, 1) * factor, -jnp.inf)
+            own_score = jnp.sum(
+                ask.astype(F32) * jnp.concatenate([k_acc[some, span]] * group, axis=0),
+                axis=-1, keepdims=True,
+            ) * factor
+            top = jnp.maximum(jnp.max(scores, axis=-1, keepdims=True), own_score)
+            expo = jnp.exp(scores - top)
+            own_expo = jnp.exp(own_score - top)
+            inverse = 1.0 / (jnp.sum(expo, axis=-1, keepdims=True) + own_expo)
+            weights = (expo * inverse).astype(BF16)
+            own_weight = (own_expo * inverse).astype(BF16).astype(F32)
+            mixed = dot(weights, vc[held, span]) + own_weight * jnp.concatenate(
+                [v_acc[some, span]] * group, axis=0
+            )
+            for h, head in enumerate(heads):
+                q_acc[some, head] = mixed[h * few:(h + 1) * few]
+        return carry
+
+    lax.fori_loop(0, docs // few, attend, 0)
+    attended[...] = q_acc[...].astype(BF16)
+
+    def project_out(step, carry):
+        output_copy(step).wait()
+        block = output_block(step)
+        part[step // n_mp, block % 2, block // 2] = dot(attended[...], wo[:, output_span(step)])
+        return carry
 
     part_near = [reduce_near(part, part_in, part_a, c) for c in range(chunks)]
     part_apart = [reduce_far(part_sum, part_far, part_b, c) for c in range(chunks)]
+    width_step = min(256, anchors, slab_rows)
+
+    def multiply(into, right):
+        def piece(step, carry):
+            span = pl.ds(pl.multiple_of(step * width_step, width_step), width_step)
+            product = dot(old_all[...].reshape(anchors, cols), right(span), 1, 1)
+            for j in range(n_mp):
+                into[j % 2, j // 2, :, span] = product[j * share:(j + 1) * share]
+            return carry
+
+        lax.fori_loop(0, into.shape[3] // width_step, piece, 0)
 
     def add_near(c):
         received([part_near[c]])
         part_sum[c] = part[c, core] + part_in[c]
         start(part_apart[c])
 
+    side_near = reduce_near(side, side_in, side_a)
+    side_apart = reduce_far(side_sum, side_far, side_b)
+    pair_near = reduce_near(pair, pair_in, pair_a)
+    pair_apart = reduce_far(pair_sum, pair_far, pair_b)
     for c in range(chunks):
-        project_out(c, 0)
+        lax.fori_loop(c * n_mp, c * n_mp + mp_half, project_out, 0)
         part_near[c].start()
-        project_out(c, mp_half)
+        lax.fori_loop(c * n_mp + mp_half, (c + 1) * n_mp, project_out, 0)
+        if c == max(chunks // 2 - 1, 0):
+            received(old_near)
+            loads[2].wait()
+            multiply(side, lambda span: sl[span])
+            side_near.start()
         if c:
             add_near(c - 1)
-
-    received(old_near)
-    loads[2].wait()
-    olds = old_all[...].reshape(anchors, cols)
-    product = dot(olds, sl[...], 1, 1)
-    for j in range(n_mp):
-        side[j % 2, j // 2] = product[j * share:(j + 1) * share]
-    side_near = reduce_near(side, side_in, side_a)
-    side_near.start()
     add_near(chunks - 1)
-    product = dot(olds, olds, 1, 1)
-    for j in range(n_mp):
-        pair[j % 2, j // 2] = product[j * share:(j + 1) * share]
-    pair_near = reduce_near(pair, pair_in, pair_a)
+    received([side_near])
+    side_sum[...] = side[core] + side_in[...]
+    start(side_apart)
+    docs_step = width_step // docs
+    multiply(
+        pair,
+        lambda span: old_all[pl.ds(span.start // docs, docs_step)].reshape(width_step, cols),
+    )
     pair_near.start()
 
     new_far = [far_rows(new_all, new_f, c) for c in range(chunks)]
@@ -331,27 +399,24 @@
     ]
     start(sq_copies)
 
-    received([side_near])
-    side_sum[...] = side[core] + side_in[...]
-    side_apart = reduce_far(side_sum, side_far, side_b)
-    start(side_apart)
-    received([pair_near])
-    pair_sum[...] = pair[core] + pair_in[...]
-    pair_apart = reduce_far(pair_sum, pair_far, pair_b)
-    start(pair_apart)
-
-    owner = owners[...]
-    chosen = jnp.where(
-        owner == lax.broadcasted_iota(jnp.int32, (n_rows, slab_rows), 0), 1.0, 0.0
-    )
-    earlier = jnp.where(
-        lax.broadcasted_iota(jnp.int32, (slab_rows, slab_rows), 0)
-        < lax.broadcasted_iota(jnp.int32, (slab_rows, slab_rows), 1), 1.0, 0.0
-    )
-    slot = jnp.sum(
-        dot(chosen.astype(BF16), earlier.astype(BF16)) * chosen, axis=0, keepdims=True
-    )
-    target = owner.astype(F32) * cap + slot
+    received(side_apart)
+    whole = side_sum[mp_slow]
+    for off in range(1, mp_half):
+        whole = whole + side_far[off - 1]
+    body = whole.astype(BF16)
+
+    def place(o, carry):
+        span = pl.ds(pl.multiple_of(o * cap, cap), cap)
+        outgoing[o] = dot(body, puts[span], 1, 1).astype(BF16)
+        return carry
+
+    lax.fori_loop(0, n_rows, place, 0)
+    trips = []
+    for off in range(1, n_rows):
+        there = lax.rem(row + off, n_rows)
+        trips.append(remote(outgoing.at[there], routed.at[mp, row], trip_sem, off - 1, mp, there))
+    start(trips)
+    routed[mp, row] = outgoing[row]
 
     received(sq_copies)
     total = sq_own[...]
@@ -365,29 +430,21 @@
     ]
     start(scale_copies)
 
+    received([pair_near])
+    pair_sum[...] = pair[core] + pair_in[...]
+    start(pair_apart)
+
     def forward(c):
         received(new_far[c])
         start(new_near[c][1:])
 
     for c in range(chunks // 2):
         forward(c)
-
-    received(side_apart)
-    whole = side_sum[mp_slow]
-    for off in range(1, mp_half):
-        whole = whole + side_far[off - 1]
-    body = whole.astype(BF16)
-    seats = lax.broadcasted_iota(jnp.int32, (cap, slab_rows), 0).astype(F32)
-    for o in range(n_rows):
-        put = jnp.where(target == seats + float(o * cap), 1.0, 0.0).astype(BF16)
-        outgoing[o] = dot(body, put, 1, 1).astype(BF16)
-    trips = []
-    for off in range(1, n_rows):
-        there = lax.rem(row + off, n_rows)
-        trips.append(remote(outgoing.at[there], routed.at[mp, row], trip_sem, off - 1, mp, there))
-    start(trips)
-    routed[mp, row] = outgoing[row]
-
+    received(trips)
+    routed_far = far_mp(routed, routed_f)
+    start(routed_far)
+    routed_near = near_mp(routed, routed_n)
+    routed_near[0].start()
     received(pair_apart)
     whole = pair_sum[mp_slow]
     for off in range(1, mp_half):
@@ -400,44 +457,58 @@
 
     for c in range(chunks // 2, chunks):
         forward(c)
-
-    received(trips)
-    routed_far = far_mp(routed, routed_f)
-    start(routed_far)
-    routed_near = near_mp(routed, routed_n)
-    routed_near[0].start()
+    received(routed_far)
+    start(routed_near[1:])
     received(gram_far)
     start(gram_near[1:])
-    received(routed_far)
-    start(routed_near[1:])
 
     received(gram_near)
     received(scale_copies)
     scale = scale_all[...].reshape(anchors, HEAD)[:, :1]
-    outs = []
-    for c in range(chunks):
-        received(new_near[c])
-        targets = new_all[c].reshape(anchors, tile).astype(F32) * scale
+    spread_scale[...] = jnp.broadcast_to(scale, spread_scale.shape)
+    row_step = min(256, n_rows * cap)
+
+    def turn_rows(b, carry):
+        span = pl.ds(pl.multiple_of(b * cap, cap), cap)
+        rows_t[span] = routed[:, b].reshape(anchors, cap).T
+        return carry
+
+    def out_copy(c):
+        span = pl.ds(pl.multiple_of(c * tile, tile), tile)
+        return pltpu.make_async_copy(staged.at[c], out.at[:, span], out_sem.at[c])
+
+    def finish(c, carry):
+        for copy in near_rows(new_all, new_n, c):
+            copy.wait_recv()
+        targets = new_all[c].reshape(anchors, tile).astype(F32) * spread_scale[:, :1]
         coeffs = solve(0.125 * D, targets, gram[...].reshape(anchors, anchors))
         top = coeffs.astype(BF16)
-        rest = (coeffs - top.astype(F32)).astype(BF16)
-        if c == 0:
-            received(routed_near)
-        for b in range(n_rows):
-            block = routed[:, b].reshape(anchors, cap)
-            staged[c, b * cap:(b + 1) * cap] = (
-                dot(block, top, 0, 0) + dot(block, rest, 0, 0)
-            ).astype(BF16)
-        outs.append(
-            pltpu.make_async_copy(
-                staged.at[c], out.at[:, c * tile:(c + 1) * tile], out_sem.at[c]
-            )
-        )
-        outs[c].start()
-    for copy in sent:
+        mapped[0] = top
+        mapped[1] = (coeffs - top.astype(F32)).astype(BF16)
+
+        @pl.when(c == 0)
+        def _():
+            for copy in routed_near:
+                copy.wait_recv()
+            lax.fori_loop(0, n_rows, turn_rows, 0)
+
+        def move(step, inner):
+            span = pl.ds(pl.multiple_of(step * row_step, row_step), row_step)
+            block = rows_t[span]
+            staged[c, span] = (dot(block, mapped[0]) + dot(block, mapped[1])).astype(BF16)
+            return inner
+
+        lax.fori_loop(0, n_rows * cap // row_step, move, 0)
+        out_copy(c).start()
+        return carry
+
+    lax.fori_loop(0, chunks, finish, 0)
+    for copy in sent + routed_near:
         copy.wait_send()
-    for copy in outs:
-        copy.wait()
+    for c in range(chunks):
+        for copy in new_near[c]:
+            copy.wait_send()
+        out_copy(c).wait()
 
 
 def local(
@@ -461,16 +532,20 @@
     chunks = cols // tile
     far_mp, far_rows = max(mp_half - 1, 1), max(rows_half - 1, 1)
     hbm = pl.BlockSpec(memory_space=pl.ANY)
-    vmem = pl.BlockSpec(memory_space=pltpu.VMEM)
     dma = pltpu.SemaphoreType.DMA
     return pl.pallas_call(
         functools.partial(encode_kernel, n_mp, n_rows),
         out_shape=jax.ShapeDtypeStruct((n_rows * cap, cols), BF16),
-        in_specs=[
-            vmem, vmem, hbm, hbm, hbm, hbm, vmem, vmem, hbm, hbm, vmem, vmem, vmem, hbm, vmem,
-        ],
-        out_specs=hbm,
+        in_specs=[hbm] * 15,
+        out_specs=pl.BlockSpec(memory_space=pl.ANY),
         scratch_shapes=[
+            pltpu.VMEM(hidden.shape, BF16),
+            pltpu.VMEM((1, width), F32),
+            pltpu.VMEM((1, HEAD), F32),
+            pltpu.VMEM((1, HEAD), F32),
+            pltpu.VMEM((1, docs), jnp.int32),
+            pltpu.VMEM((1, width), F32),
+            pltpu.VMEM((1, slab_rows), jnp.int32),
             pltpu.VMEM((width, q_width), BF16),
             pltpu.VMEM((width, kv_width), BF16),
             pltpu.VMEM((width, kv_width), BF16),
@@ -503,8 +578,13 @@
             pltpu.VMEM((n_rows, share, cap), BF16),
             pltpu.VMEM((n_mp, n_rows, share, cap), BF16),
             pltpu.VMEM((n_mp, share, anchors), F32),
+            pltpu.VMEM((docs, 128), F32),
+            pltpu.VMEM((anchors, 128), F32),
+            pltpu.VMEM((2, anchors, tile), BF16),
+            pltpu.VMEM((n_rows * cap, anchors), BF16),
+            pltpu.VMEM((n_rows * cap, slab_rows), BF16),
             pltpu.VMEM((chunks, n_rows * cap, tile), BF16),
-            dma((3,)), dma((3, CHUNKS)), dma((n_mp * chunks,)),
+            dma((11,)), dma((3, CHUNKS)), dma((n_mp * chunks,)),
             dma((2, chunks, 1)), dma((2, chunks, far_mp)), dma((2, n_mp - 1)),
             dma((2, n_rows - 1)),
             dma((2, chunks, far_rows)), dma((2, chunks, rows_half)),
@@ -517,7 +597,7 @@
             dma((chunks,)),
         ],
         compiler_params=pltpu.CompilerParams(
-            collective_id=0, has_side_effects=True, vmem_limit_bytes=56 * 2**20
+            collective_id=0, has_side_effects=True, vmem_limit_bytes=60 * 2**20
         ),
         name="encode",
     )(

time: 51.6 us -> 59 us (1.14)
  Pallas kernels: 47.8 us -> 55.7 us
    pallas_call x1, Pallas kernels: 47.8 us -> 55.7 us  [local(): pl.pallas_call(functools.partial(encode_kernel, n_mp, n_rows), out_shape=...]
where the time goes in v3:
time: 59 us; the launch traced here: 58.8 us
  Pallas kernels  55.7 us (94%)
  local copies, waits for them, and re-layouts  3.08 us (5%)
    pallas_call x1, Pallas kernels, local(): pl.pallas_call(functools.partial(encode_kernel, n_mp, n_rows), out_shape=...  55.7 us
    unnamed x1, local copies, waits for them, and re-layouts  3.08 us

profile of v3, /device:TPU:1, one launch (start us, length us, event | category | flops | bytes accessed | tf_op | source)
XLA Modules:
  0.0 58.8 jit_solution(13570597947522727131)
XLA Ops:
  0.0 55.7 %encode.1 = bf16[1024,1024]{1,0:T(8,128)(2,1)} custom-call(bf16[32,4096]{1,0:T(8,128)(2,1)} %hidden_in.1, f32[1,4096]{1,0:T(1,128)} %bitcast.10, bf16[4096,1024]{1,0:T(8,128)(2,1)} %w_query.1, bf16[4096,256]{1,0:T(8,128)(2,1)} %w_key.1, bf16[4096,256]{1,0:T(8,128)(2,1)} %w_value.1, bf16[1024,4096]{1,0:T(8,128)(2,1)} %w_output.1, f32[1,128]{1,0:T(1,128)} %bitcast.13, ...), custom_call_target="tpu_custom_call" | custom-call | tf_op jit(solution)/shard_map/encode/pallas_call | solution.py:536
  55.7 3.1 %copy.17 = bf16[1024,1024]{1,0:T(8,128)(2,1)} copy(bf16[1024,1024]{1,0:T(8,128)(2,1)} %encode.1) | data formatting | bytes 4194304

commit v4 on v3

--- a/solution.py
+++ b/solution.py
@@ -61,14 +61,14 @@
     n_mp, n_rows,
     hidden_in, attn_gain_in, w_query, w_key, w_value, w_output, query_gain_in, key_gain_in,
     key_cache, value_cache, lengths_in, final_gain_in, old_embed, slab, owners_in,
-    out,
+    coeffs_out, rows_out,
     hidden, attn_gain, query_gain, key_gain, lengths, final_gain, owners,
     wq, wk, wv, wo, kc, vc, sl, normed, q_acc, k_acc, v_acc, attended,
     part, part_in, part_sum, part_far, sq_own, sq_in, scale_all, new_all,
     old_all, side, side_in, side_sum, side_far, pair, pair_in, pair_sum, pair_far,
-    outgoing, routed, gram, spread_length, spread_scale, mapped, rows_t, puts, staged,
+    outgoing, routed, gram, spread_scale, mapped, rows_t, puts,
     load_sem, weight_sem, wo_sem,
-    part_a, part_b, sq_sem, scale_sem, new_f, new_n, old_f, old_n,
+    part_a, part_b, sq_sem, scale_sem, new_f, new_n, old_d,
     side_a, side_b, pair_a, pair_b,
     trip_sem, gram_f, gram_n, routed_f, routed_n, out_sem,
 ):
@@ -206,10 +206,11 @@
         copy.wait()
     pl.semaphore_wait(barrier, n_rows + n_mp - 2)
 
-    old_far = far_rows(old_all, old_f)
-    start(old_far)
-    old_near = near_rows(old_all, old_n)
-    old_near[0].start()
+    old_direct = [
+        remote(old_all.at[row], old_all.at[row], old_d, off - 1, mp, lax.rem(row + off, n_rows))
+        for off in range(1, n_rows)
+    ]
+    start(old_direct)
 
     q_acc[...] = jnp.zeros_like(q_acc)
     k_acc[...] = jnp.zeros_like(k_acc)
@@ -248,14 +249,7 @@
         v_acc[...] += dot(piece, wv[span, :])
         return carry
 
-    done = CHUNKS // 2
-    lax.fori_loop(0, done, project, 0)
-    for off in range(1, rows_half):
-        lax.fori_loop(done, max(done, CHUNKS * (rows_half + off) // (2 * rows_half)), project, 0)
-        done = max(done, CHUNKS * (rows_half + off) // (2 * rows_half))
-        received(old_far[off - 1:off])
-        old_near[off].start()
-    lax.fori_loop(done, CHUNKS, project, 0)
+    lax.fori_loop(0, CHUNKS, project, 0)
 
     spot = lax.broadcasted_iota(jnp.int32, (docs, docs), 0)
     named = lax.broadcasted_iota(jnp.int32, (docs, docs), 1)
@@ -283,33 +277,24 @@
     place_row = lax.broadcasted_iota(jnp.int32, (tall, wide), 0) % few * ctx
     place_lane = lax.broadcasted_iota(jnp.int32, (tall, wide), 1)
     factor = 1.0 / math.sqrt(HEAD)
-    spread_length[...] = jnp.broadcast_to(length, spread_length.shape)
-
-    def turn_query(h, carry):
-        span = pl.ds(pl.multiple_of(h * HEAD, HEAD), HEAD)
-        q_acc[:, span] = turned(q_acc[:, span], query_gain[...])
-        return carry
-
-    lax.fori_loop(0, kv_local * group, turn_query, 0)
     for g in range(kv_local):
         span = slice(g * HEAD, (g + 1) * HEAD)
-        k_acc[:, span] = turned(k_acc[:, span], key_gain[...]).astype(BF16).astype(F32)
-    v_acc[...] = v_acc[...].astype(BF16).astype(F32)
-
-    def attend(block, carry):
-        some = pl.ds(pl.multiple_of(block * few, few), few)
-        held = pl.ds(pl.multiple_of(block * few * ctx, few * ctx), few * ctx)
-        long = jnp.concatenate([spread_length[some, :1]] * group, axis=0).astype(jnp.int32)
-        valid = (place_lane >= place_row) & (place_lane < place_row + long)
-        for g in range(kv_local):
-            span = slice(g * HEAD, (g + 1) * HEAD)
-            heads = [
-                slice((g * group + h) * HEAD, (g * group + h + 1) * HEAD) for h in range(group)
-            ]
-            ask = jnp.concatenate([q_acc[some, head] for head in heads], axis=0).astype(BF16)
+        queries = [
+            turned(q_acc[:, (g * group + h) * HEAD:(g * group + h + 1) * HEAD], query_gain[...])
+            for h in range(group)
+        ]
+        key_new = turned(k_acc[:, span], key_gain[...]).astype(BF16).astype(F32)
+        value_new = v_acc[:, span].astype(BF16).astype(F32)
+        mixed = []
+        for first in range(0, docs, few):
+            some = slice(first, first + few)
+            ask = jnp.concatenate([query[some] for query in queries], axis=0).astype(BF16)
+            long = jnp.concatenate([length[some]] * group, axis=0).astype(jnp.int32)
+            valid = (place_lane >= place_row) & (place_lane < place_row + long)
+            held = slice(first * ctx, (first + few) * ctx)
             scores = jnp.where(valid, dot(ask, kc[held, span], 1, 1) * factor, -jnp.inf)
             own_score = jnp.sum(
-                ask.astype(F32) * jnp.concatenate([k_acc[some, span]] * group, axis=0),
+                ask.astype(F32) * jnp.concatenate([key_new[some]] * group, axis=0),
                 axis=-1, keepdims=True,
             ) * factor
             top = jnp.maximum(jnp.max(scores, axis=-1, keepdims=True), own_score)
@@ -318,15 +303,14 @@
             inverse = 1.0 / (jnp.sum(expo, axis=-1, keepdims=True) + own_expo)
             weights = (expo * inverse).astype(BF16)
             own_weight = (own_expo * inverse).astype(BF16).astype(F32)
-            mixed = dot(weights, vc[held, span]) + own_weight * jnp.concatenate(
-                [v_acc[some, span]] * group, axis=0
+            mixed.append(
+                dot(weights, vc[held, span])
+                + own_weight * jnp.concatenate([value_new[some]] * group, axis=0)
             )
-            for h, head in enumerate(heads):
-                q_acc[some, head] = mixed[h * few:(h + 1) * few]
-        return carry
-
-    lax.fori_loop(0, docs // few, attend, 0)
-    attended[...] = q_acc[...].astype(BF16)
+        for h in range(group):
+            attended[:, (g * group + h) * HEAD:(g * group + h + 1) * HEAD] = jnp.concatenate(
+                [block[h * few:(h + 1) * few] for block in mixed], axis=0
+            ).astype(BF16)
 
     def project_out(step, carry):
         output_copy(step).wait()
@@ -361,23 +345,22 @@
         lax.fori_loop(c * n_mp, c * n_mp + mp_half, project_out, 0)
         part_near[c].start()
         lax.fori_loop(c * n_mp + mp_half, (c + 1) * n_mp, project_out, 0)
-        if c == max(chunks // 2 - 1, 0):
-            received(old_near)
-            loads[2].wait()
-            multiply(side, lambda span: sl[span])
-            side_near.start()
         if c:
             add_near(c - 1)
     add_near(chunks - 1)
-    received([side_near])
-    side_sum[...] = side[core] + side_in[...]
-    start(side_apart)
+    received(old_direct)
+    loads[2].wait()
+    multiply(side, lambda span: sl[span])
+    side_near.start()
     docs_step = width_step // docs
     multiply(
         pair,
         lambda span: old_all[pl.ds(span.start // docs, docs_step)].reshape(width_step, cols),
     )
     pair_near.start()
+    received([side_near])
+    side_sum[...] = side[core] + side_in[...]
+    start(side_apart)
 
     new_far = [far_rows(new_all, new_f, c) for c in range(chunks)]
     new_near = [near_rows(new_all, new_n, c) for c in range(chunks)]
@@ -405,12 +388,8 @@
         whole = whole + side_far[off - 1]
     body = whole.astype(BF16)
 
-    def place(o, carry):
-        span = pl.ds(pl.multiple_of(o * cap, cap), cap)
-        outgoing[o] = dot(body, puts[span], 1, 1).astype(BF16)
-        return carry
-
-    lax.fori_loop(0, n_rows, place, 0)
+    for o in range(n_rows):
+        outgoing[o] = dot(body, puts[o * cap:(o + 1) * cap], 1, 1).astype(BF16)
     trips = []
     for off in range(1, n_rows):
         there = lax.rem(row + off, n_rows)
@@ -466,40 +445,32 @@
     received(scale_copies)
     scale = scale_all[...].reshape(anchors, HEAD)[:, :1]
     spread_scale[...] = jnp.broadcast_to(scale, spread_scale.shape)
-    row_step = min(256, n_rows * cap)
+    rows_copy = pltpu.make_async_copy(rows_t, rows_out, out_sem.at[chunks])
 
     def turn_rows(b, carry):
         span = pl.ds(pl.multiple_of(b * cap, cap), cap)
         rows_t[span] = routed[:, b].reshape(anchors, cap).T
         return carry
 
-    def out_copy(c):
-        span = pl.ds(pl.multiple_of(c * tile, tile), tile)
-        return pltpu.make_async_copy(staged.at[c], out.at[:, span], out_sem.at[c])
+    def coeffs_copy(c):
+        return pltpu.make_async_copy(mapped.at[c], coeffs_out.at[c], out_sem.at[c])
 
     def finish(c, carry):
+        @pl.when(c == chunks - 1)
+        def _():
+            for copy in routed_near:
+                copy.wait_recv()
+            lax.fori_loop(0, n_rows, turn_rows, 0)
+            rows_copy.start()
+
         for copy in near_rows(new_all, new_n, c):
             copy.wait_recv()
         targets = new_all[c].reshape(anchors, tile).astype(F32) * spread_scale[:, :1]
         coeffs = solve(0.125 * D, targets, gram[...].reshape(anchors, anchors))
         top = coeffs.astype(BF16)
-        mapped[0] = top
-        mapped[1] = (coeffs - top.astype(F32)).astype(BF16)
-
-        @pl.when(c == 0)
-        def _():
-            for copy in routed_near:
-                copy.wait_recv()
-            lax.fori_loop(0, n_rows, turn_rows, 0)
-
-        def move(step, inner):
-            span = pl.ds(pl.multiple_of(step * row_step, row_step), row_step)
-            block = rows_t[span]
-            staged[c, span] = (dot(block, mapped[0]) + dot(block, mapped[1])).astype(BF16)
-            return inner
-
-        lax.fori_loop(0, n_rows * cap // row_step, move, 0)
-        out_copy(c).start()
+        mapped[c, 0] = top
+        mapped[c, 1] = (coeffs - top.astype(F32)).astype(BF16)
+        coeffs_copy(c).start()
         return carry
 
     lax.fori_loop(0, chunks, finish, 0)
@@ -508,7 +479,12 @@
     for c in range(chunks):
         for copy in new_near[c]:
             copy.wait_send()
-        out_copy(c).wait()
+        coeffs_copy(c).wait()
+    rows_copy.wait()
+
+
+def apply_kernel(rows, coeffs, out):
+    out[...] = (dot(rows[...], coeffs[0, 0]) + dot(rows[...], coeffs[0, 1])).astype(BF16)
 
 
 def local(
@@ -533,11 +509,14 @@
     far_mp, far_rows = max(mp_half - 1, 1), max(rows_half - 1, 1)
     hbm = pl.BlockSpec(memory_space=pl.ANY)
     dma = pltpu.SemaphoreType.DMA
-    return pl.pallas_call(
+    coeffs, rows = pl.pallas_call(
         functools.partial(encode_kernel, n_mp, n_rows),
-        out_shape=jax.ShapeDtypeStruct((n_rows * cap, cols), BF16),
+        out_shape=(
+            jax.ShapeDtypeStruct((chunks, 2, anchors, tile), BF16),
+            jax.ShapeDtypeStruct((n_rows * cap, anchors), BF16),
+        ),
         in_specs=[hbm] * 15,
-        out_specs=pl.BlockSpec(memory_space=pl.ANY),
+        out_specs=(hbm, hbm),
         scratch_shapes=[
             pltpu.VMEM(hidden.shape, BF16),
             pltpu.VMEM((1, width), F32),
@@ -578,23 +557,21 @@
             pltpu.VMEM((n_rows, share, cap), BF16),
             pltpu.VMEM((n_mp, n_rows, share, cap), BF16),
             pltpu.VMEM((n_mp, share, anchors), F32),
-            pltpu.VMEM((docs, 128), F32),
             pltpu.VMEM((anchors, 128), F32),
-            pltpu.VMEM((2, anchors, tile), BF16),
+            pltpu.VMEM((chunks, 2, anchors, tile), BF16),
             pltpu.VMEM((n_rows * cap, anchors), BF16),
             pltpu.VMEM((n_rows * cap, slab_rows), BF16),
-            pltpu.VMEM((chunks, n_rows * cap, tile), BF16),
             dma((11,)), dma((3, CHUNKS)), dma((n_mp * chunks,)),
             dma((2, chunks, 1)), dma((2, chunks, far_mp)), dma((2, n_mp - 1)),
             dma((2, n_rows - 1)),
             dma((2, chunks, far_rows)), dma((2, chunks, rows_half)),
-            dma((2, far_rows)), dma((2, rows_half)),
+            dma((2, n_rows - 1)),
             dma((2, 1)), dma((2, far_mp)),
             dma((2, 1)), dma((2, far_mp)),
             dma((2, n_rows - 1)),
             dma((2, far_mp)), dma((2, mp_half)),
             dma((2, far_mp)), dma((2, mp_half)),
-            dma((chunks,)),
+            dma((chunks + 1,)),
         ],
         compiler_params=pltpu.CompilerParams(
             collective_id=0, has_side_effects=True, vmem_limit_bytes=60 * 2**20
@@ -605,6 +582,18 @@
         query_gain.reshape(1, -1), key_gain.reshape(1, -1), key_cache, value_cache,
         lengths.reshape(1, -1), final_gain.reshape(1, -1), old_embed, slab, owners.reshape(1, -1),
     )
+    return pl.pallas_call(
+        apply_kernel,
+        out_shape=jax.ShapeDtypeStruct((n_rows * cap, cols), BF16),
+        grid=(chunks,),
+        in_specs=[
+            pl.BlockSpec((n_rows * cap, anchors), lambda i: (0, 0)),
+            pl.BlockSpec((1, 2, anchors, tile), lambda i: (i, 0, 0, 0)),
+        ],
+        out_specs=pl.BlockSpec((n_rows * cap, tile), lambda i: (0, i)),
+        compiler_params=pltpu.CompilerParams(vmem_limit_bytes=60 * 2**20),
+        name="apply",
+    )(rows, coeffs)
 
 def solution(mesh):
     return jax.shard_map(

time: 59 us -> 53.7 us (0.910)
  local copies, waits for them, and re-layouts: 3.08 us -> 0 us
  Pallas kernels: 55.7 us -> 53 us
    pallas_call x1, Pallas kernels: 55.7 us -> 48.4 us  [local(): pl.pallas_call(functools.partial(encode_kernel, n_mp, n_rows), out_shape=...]
    pallas_call x0 -> x1, Pallas kernels: none -> 4.56 us  [local(): pl.pallas_call(apply_kernel, out_shape=jax.ShapeDtypeStruct((n_rows * cap...]
    unnamed x1 -> x0, local copies, waits for them, and re-layouts: 3.08 us -> none
where the time goes in v4:
time: 53.7 us; the launch traced here: 53 us
  Pallas kernels  53 us (99%)
    pallas_call x1, Pallas kernels, local(): pl.pallas_call(functools.partial(encode_kernel, n_mp, n_rows), out_shape=...  48.4 us
    pallas_call x1, Pallas kernels, local(): pl.pallas_call(apply_kernel, out_shape=jax.ShapeDtypeStruct((n_rows * cap...  4.56 us

profile of v4, /device:TPU:1, one launch (start us, length us, event | category | flops | bytes accessed | tf_op | source)
XLA Modules:
  0.0 53.0 jit_solution(318436048839573510)
XLA Ops:
  0.0 48.4 %encode.1 = (bf16[4,2,256,256]{3,2,1,0:T(8,128)(2,1)}, bf16[1024,256]{1,0:T(8,128)(2,1)}) custom-call(bf16[32,4096]{1,0:T(8,128)(2,1)} %hidden_in.1, f32[1,4096]{1,0:T(1,128)} %bitcast.10, bf16[4096,1024]{1,0:T(8,128)(2,1)} %w_query.1, bf16[4096,256]{1,0:T(8,128)(2,1)} %w_key.1, bf16[4096,256]{1,0:T(8,128)(2,1)} %w_value.1, bf16[1024,4096]{1,0:T(8,128)(2,1)} %w_output.1, ...), custom_call_target="tpu_custom_call" | custom-call | tf_op jit(solution)/shard_map/encode/pallas_call | solution.py:512
  48.5 4.6 %apply.1 = bf16[1024,1024]{1,0:T(8,128)(2,1)} custom-call(bf16[1024,256]{1,0:T(8,128)(2,1)} %get-tuple-element.7.rows, bf16[4,2,256,256]{3,2,1,0:T(8,128)(2,1)} %get-tuple-element.8.coeffs), custom_call_target="tpu_custom_call" | custom-call | tf_op jit(solution)/shard_map/apply/pallas_call | solution.py:585
